TPU v7x, 32 devices: a whole 2x2x4 slice. The times are simulated.
32 devices in a mesh: groups: 2 (over y), tensor: 4 (over z), batch: 4 (over x, core).
Axes of the slice: x: 2, y: 2, z: 4, core: 2. Of those that a mesh axis runs over, the one named last changes fastest.
Arguments:
- stream: bfloat16 [1024, 12288], P(('groups', 'batch'), 'tensor'), parts along dimension 0, may hold values from -6 to 6
- ln_gain: bfloat16 [12288], replicated, may hold values from 0.099609375 to 1.8984375
- ln_bias: bfloat16 [12288], replicated, may hold values from -3 to 3
- fc1_weight: bfloat16 [12288, 24576], P('batch', 'tensor'), may hold values from -0.0546875 to 0.0546875
- fc1_bias: bfloat16 [24576], P('tensor'), may hold values from -3 to 3
- fc2_weight: bfloat16 [24576, 12288], P('tensor', 'batch'), may hold values from -0.25 to 0.25
- fc2_bias: bfloat16 [12288], P('tensor'), may hold values from -3 to 3
- active_ids: int32 [8, 16], P('groups'), parts along dimension 0, may hold values from 0 to 191, as said below
- active_counts: int32 [8], P('groups'), parts along dimension 0, may hold values from 4 to 16
Outputs:
- mixed: bfloat16 [1024, 12288], P(('groups', 'batch'), 'tensor'), parts along dimension 0
There are 2 independent parts, one for each index of `groups`. A program takes and returns all parts, laid end to end along the dimension named above; an argument that names none is the same for every part. Nothing has to cross between parts.
Inputs may be any that keep to these rules, and one draw needn't show every extreme that they name: `active_ids`: the first active_counts[r] entries of row r are distinct block numbers; among them at most 4 lie in any range of 48 consecutive blocks starting at a multiple of it, and in every row batch some such range holds exactly 4. Entries after the count are arbitrary block numbers.
All inputs are finite; a program needn't handle non-finite values.
Results may differ from a plain program's by a relative error of at most 0.0051.
Values may be sent and summed in bfloat16 or wider, within the bound.
No kernel may reach another device: no remote copies, remote signals or barrier semaphores. Data moves between devices by JAX's collectives and lax.ppermute only.
A program may use at most 320 MiB of HBM per device.

v0:
```python
import jax
import jax.numpy as jnp
from jax import lax
from jax.sharding import PartitionSpec as P

BLOCK = 128
CAP = 4


def normalize(values_in, gain, shift):
    values = values_in.astype(jnp.float32)
    center = jnp.mean(values, axis=-1, keepdims=True)
    spread = jnp.mean(jnp.square(values - center), axis=-1, keepdims=True)
    scaled = (values - center) * lax.rsqrt(spread + 1e-05)
    return (scaled * gain.astype(jnp.float32) + shift.astype(jnp.float32)).astype(jnp.bfloat16)


def shards(
    stream, ln_gain, ln_bias, fc1_weight, fc1_bias, fc2_weight, fc2_bias, active_ids, active_counts
):
    batches = lax.axis_size("batch")
    tensor_index = lax.axis_index("tensor")
    whole_rows = lax.all_gather(stream, "tensor", axis=1, tiled=True)
    normed = normalize(whole_rows, ln_gain, ln_bias)
    columns = lax.all_to_all(normed, "batch", split_axis=1, concat_axis=0, tiled=True)
    row_total = stream.shape[0]
    width_part = columns.shape[1]
    local_blocks = fc1_weight.shape[1] // BLOCK
    slot_total = active_ids.shape[1]
    local_ids = active_ids - tensor_index * local_blocks
    present = (
        (jnp.arange(slot_total)[None, :] < active_counts[:, None])
        & (local_ids >= 0)
        & (local_ids < local_blocks)
    )
    present_int = present.astype(jnp.int32)
    position = jnp.cumsum(present_int, axis=1) - 1
    matches = present_int[:, :, None] * (
        position[:, :, None] == jnp.arange(CAP)[None, None, :]
    ).astype(jnp.int32)
    slot_block = jnp.sum(matches * local_ids[:, :, None], axis=1)
    slot_live = jnp.sum(matches, axis=1).astype(jnp.float32)
    grouped_rows = columns.reshape(batches, row_total, width_part)
    bias_table = fc1_bias.reshape(local_blocks, BLOCK).astype(jnp.float32)
    slot_bias = jnp.take(bias_table, slot_block, axis=0)
    up_taken = jnp.take(fc1_weight.reshape(width_part, local_blocks, BLOCK), slot_block, axis=1)
    partial_value = jnp.einsum(
        "rnd,drck->rnck", grouped_rows, up_taken, preferred_element_type=jnp.float32
    )
    my_share = lax.psum_scatter(partial_value, "batch", scatter_dimension=0, tiled=True)
    batch_index = lax.axis_index("batch")
    my_bias = lax.dynamic_slice_in_dim(slot_bias, batch_index, 1, 0)
    my_live = lax.dynamic_slice_in_dim(slot_live, batch_index, 1, 0)
    my_hidden = (jnp.maximum(my_share + my_bias[:, None], 0.0) * my_live[:, None, :, None]).astype(
        jnp.bfloat16
    )
    hidden_state = lax.all_gather(my_hidden, "batch", axis=0, tiled=True)
    down_width = fc2_weight.shape[1]
    down_taken = jnp.take(fc2_weight.reshape(local_blocks, BLOCK, down_width), slot_block, axis=0)
    partial_out = jnp.einsum(
        "rnck,rcke->rne", hidden_state, down_taken, preferred_element_type=jnp.float32
    )
    partial_out = partial_out.reshape(batches * row_total, down_width)
    returned = lax.all_to_all(partial_out, "batch", split_axis=0, concat_axis=1, tiled=True)
    summed = lax.psum_scatter(returned, "tensor", scatter_dimension=1, tiled=True)
    return (stream.astype(jnp.float32) + summed + fc2_bias.astype(jnp.float32)).astype(jnp.bfloat16)


def solution(mesh):
    in_specs = (
        P(("groups", "batch"), "tensor"),
        P(),
        P(),
        P("batch", "tensor"),
        P("tensor"),
        P("tensor", "batch"),
        P("tensor"),
        P("groups", None),
        P("groups"),
    )
    out_specs = P(("groups", "batch"), "tensor")
    return jax.shard_map(shards, mesh=mesh, in_specs=in_specs, out_specs=out_specs, check_vma=False)
```

profile of v0, /device:TPU:0, one launch (start us, length us, event | category | flops | bytes accessed | tf_op | source)
XLA Modules:
  0.0 449.9 jit_solution(6229389048461646813)
XLA Ops:
  6.5 0.0 all-gather.2.cloned.1.call-start
  6.5 2.3 copy.32
  8.8 0.0 all-gather.2.cloned.1.call-update
  8.8 0.7 convert_element_type.40
  9.6 0.7 convert_element_type.39
  10.3 64.9 %all-gather.2.cloned.1.call-done = bf16[128,12288]{0,1:T(8,128)(2,1)} async-done(((bf16[128,3072]{0,1:T(8,128)(2,1)}), bf16[128,12288]{0,1:T(8,128)(2,1)}) %all-gather.2.cloned.1.call-update) | async-done | bytes 3145744 | tf_op jit(solution)/shard_map/all_gather | solution.py:23
  75.2 0.0 copy-start
  75.2 3.2 convert_reduce_fusion
  78.4 3.1 fusion.9
  81.5 0.0 copy-done
  81.5 6.6 %fusion.12 = bf16[128,12288]{0,1:T(8,128)(2,1)S(1)} fusion(bf16[128,12288]{0,1:T(8,128)(2,1)S(1)} %copy-done, f32[12288]{0:T(1024)S(1)} %convert_element_type.40, f32[12288]{0:T(1024)S(1)} %convert_element_type.39, f32[128]{0:T(128)S(1)} %add_rsqrt_fusion, f32[128]{0:T(128)S(1)} %broadcast_multiply_fusion), kind=kLoop, calls=%fused_computation.17 | loop fusion | flops 9437184 | bytes 6390784 | tf_op jit(solution)/shard_map/convert_element_type | solution.py:15
  88.1 2.8 copy.34
  91.0 3.7 all-to-all-start
  94.7 0.0 reduce-scatter.3.cloned.1.call-start
  94.7 48.7 %copy.35 = bf16[3072,6144]{0,1:T(8,128)(2,1)} copy(bf16[3072,6144]{1,0:T(8,128)(2,1)} %param.12) | data formatting | bytes 75497472 | tf_op args[3]
  143.4 0.0 copy-start.4
  143.4 0.0 copy-start.5
  143.4 48.6 %copy.36 = bf16[3072,48,128]{2,0,1:T(8,128)(2,1)} copy(bf16[3072,48,128]{0,2,1:T(8,128)(2,1)} %bitcast.33) | data formatting | bytes 75497472 | tf_op jit(solution)/shard_map/reshape | solution.py:46
  192.0 0.0 copy-done.4
  192.0 0.0 copy-done.5
  192.0 0.1 fusion.23
  192.0 0.2 reduce_window_sum.11
  192.2 0.2 select_reduce_fusion
  192.5 0.1 reshape.73
  192.6 9.9 %gather_fusion = bf16[16,3072,128]{2,1,0:T(8,128)(2,1)} fusion(bf16[3072,48,128]{2,0,1:T(8,128)(2,1)} %copy.36, s32[1024]{0:T(1024)S(1)} %pad_clamp_fusion), kind=kCustom, calls=%fused_computation | custom fusion | bytes 25165888 | tf_op jit(solution)/shard_map/jit(_take)/gather | solution.py:46
  202.4 0.0 all-to-all-done
  202.5 0.0 copy-start.2
  202.5 8.0 %fusion = f32[4,128,4,128]{3,1,2,0:T(8,128)} fusion(bf16[4,4,3072,128]{3,2,1,0:T(8,128)(2,1)} %bitcast.37, pred[4,4]{1,0:T(4,128)(4,1)S(1)} %compare_and_fusion, bf16[128,4,3072]{2,0,1:T(8,128)(2,1)S(1)} %all-to-all-done), kind=kOutput, calls=%fused_computation.3 | convolution fusion | flops 1616904192 | bytes 16777232 | tf_op jit(solution)/shard_map/rnd,drck->rnck/dot_general | solution.py:47
  210.5 0.0 reduce-scatter.3.cloned.1.call-update
  210.5 0.0 reduce-scatter.5.cloned.1.call-start
  210.6 0.0 copy-done.2
  210.6 0.6 gather_fusion.1
  211.2 10.3 %gather_fusion.2 = bf16[16,128,3072]{2,1,0:T(8,128)(2,1)} fusion(bf16[48,128,3072]{2,1,0:T(8,128)(2,1)} %bitcast.39, s32[1024]{0:T(1024)S(1)} %pad_clamp_fusion), kind=kCustom, calls=%fused_computation.2 | custom fusion | bytes 25165888 | tf_op jit(solution)/shard_map/jit(_take)/gather | solution.py:59
  221.5 0.1 fusion.20
  221.5 13.4 %reduce-scatter.3.cloned.1.call-done = f32[1,128,4,128]{3,1,2,0:T(8,128)} async-done(((f32[4,128,4,128]{3,1,2,0:T(8,128)}), f32[1,128,4,128]{3,1,2,0:T(8,128)}) %reduce-scatter.3.cloned.1.call-update) | async-done | bytes 262160 | tf_op jit(solution)/shard_map/reduce_scatter | solution.py:50
  234.9 1.0 multiply_convert_fusion
  235.9 6.8 %all_gather.7 = bf16[4,128,4,128]{3,1,2,0:T(8,128)(2,1)S(1)} all-gather(bf16[1,128,4,128]{3,1,2,0:T(8,128)(2,1)S(1)} %multiply_convert_fusion), channel_id=1, replica_groups=mesh['groups'=2,'tensor'=4,'batch'=4] {'batch'}, dimensions={0}, use_global_device_ids=true | all-gather | bytes 655360 | tf_op jit(solution)/shard_map/all_gather | solution.py:57
  242.7 5.8 %fusion.15 = f32[4,128,3072]{2,1,0:T(8,128)S(1)} fusion(bf16[4,128,4,128]{3,1,2,0:T(8,128)(2,1)S(1)} %all_gather.7, bf16[4,4,128,3072]{3,2,1,0:T(8,128)(2,1)} %bitcast.36, pred[4,4]{1,0:T(4,128)(4,1)S(1)} %compare_and_fusion), kind=kOutput, calls=%fused_computation.20 | convolution fusion | flops 1616904192 | bytes 19398672 | tf_op jit(solution)/shard_map/rnck,rcke->rne/dot_general | solution.py:60
  248.5 74.2 %all_to_all.32 = f32[4,128,3072]{2,1,0:T(8,128)} all-to-all(f32[4,128,3072]{2,1,0:T(8,128)S(1)} %fusion.15), channel_id=1, replica_groups=mesh['groups'=2,'tensor'=4,'batch'=4] {'batch'}, dimensions={0} | all-to-all | bytes 12582912 | tf_op jit(solution)/shard_map/all_to_all | solution.py:64
  322.8 6.6 %copy.37 = f32[128,4,3072]{0,2,1:T(8,128)} copy(f32[128,4,3072]{2,0,1:T(8,128)} %bitcast.35) | data formatting | bytes 12582912 | tf_op jit(solution)/shard_map/all_to_all | solution.py:64
  329.4 0.0 copy-start.3
  329.4 0.0 copy-start.1
  329.4 0.0 reduce-scatter.5.cloned.1.call-update
  329.4 0.7 copy-done.3
  330.0 110.3 %reduce-scatter.5.cloned.1.call-done = f32[128,3072]{0,1:T(8,128)} async-done(((f32[128,12288]{0,1:T(8,128)}), f32[128,3072]{0,1:T(8,128)}) %reduce-scatter.5.cloned.1.call-update) | async-done | bytes 1572880 | tf_op jit(solution)/shard_map/reduce_scatter | solution.py:65
  440.3 0.0 copy-done.1
  440.3 1.9 add_convert_fusion
  442.2 1.2 copy.38
  (11 shorter events, 0.1 us)
Async XLA Ops:
  6.5 68.7 %all-gather.2.cloned.1.call-start = ((), (), s32[]{:S(2)}) async-start(), calls=%async_computation.4 | async-start | bytes 3932160 | tf_op jit(solution)/shard_map/all_gather | solution.py:23
  75.2 6.3 %copy-start = (bf16[128,12288]{0,1:T(8,128)(2,1)S(1)}, bf16[128,12288]{0,1:T(8,128)(2,1)}, u32[]{:S(2)}) copy-start(bf16[128,12288]{0,1:T(8,128)(2,1)} %all-gather.2.cloned.1.call-done) | copy-start | bytes 9437188
  91.0 111.5 %all-to-all-start = ((bf16[128,4,3072]{2,0,1:T(8,128)(2,1)}), bf16[128,4,3072]{2,0,1:T(8,128)(2,1)S(1)}, u32[]{:S(2)}, u32[]{:S(2)}) async-start(bf16[128,4,3072]{2,0,1:T(8,128)(2,1)} %copy.34), calls=%async_computation | async-start | bytes 6291456 | tf_op jit(solution)/shard_map/all_to_all | solution.py:25
  94.7 140.2 %reduce-scatter.3.cloned.1.call-start = ((), (), s32[]{:S(2)}) async-start(), calls=%async_computation.5 | async-start | bytes 1310720 | tf_op jit(solution)/shard_map/reduce_scatter | solution.py:50
  143.4 48.6 %copy-start.4 = (s32[4,16]{1,0:T(4,128)S(1)}, s32[4,16]{1,0:T(4,128)}, u32[]{:S(2)}) copy-start(s32[4,16]{1,0:T(4,128)} %param.16) | copy-start | bytes 772
  143.4 48.6 %copy-start.5 = (s32[4]{0:T(128)S(1)}, s32[4]{0:T(128)}, u32[]{:S(2)}) copy-start(s32[4]{0:T(128)} %param.17) | copy-start | bytes 52
  202.5 8.1 %copy-start.2 = (bf16[6144]{0:T(1024)(128)(2,1)S(1)}, bf16[6144]{0:T(1024)(128)(2,1)}, u32[]{:S(2)}) copy-start(bf16[6144]{0:T(1024)(128)(2,1)} %param.13) | copy-start | bytes 36868
  210.5 229.8 %reduce-scatter.5.cloned.1.call-start = ((), (), s32[]{:S(2)}) async-start(), calls=%async_computation.6 | async-start | bytes 7864320 | tf_op jit(solution)/shard_map/reduce_scatter | solution.py:65
  329.4 0.7 copy-start.3
  329.4 111.0 %copy-start.1 = (bf16[128,3072]{0,1:T(8,128)(2,1)S(1)}, bf16[128,3072]{0,1:T(8,128)(2,1)}, u32[]{:S(2)}) copy-start(bf16[128,3072]{0,1:T(8,128)(2,1)} %copy.32) | copy-start | bytes 2359300
Sparse Core Ops, SparseCore 0:
  9.0 66.1 all-gather.1
  210.6 24.2 reduce-scatter.2
  329.5 110.7 reduce-scatter.4
where the time goes:
time: 453 us; the launch traced here: 450 us
  waiting for transfers between devices  189 us (42%)
  local copies, waits for them, and re-layouts  132 us (29%)
  blocking collectives  81 us (18%)
  other arithmetic  17.9 us (4%)
  matrix products  13.8 us (3%)
  between operations  13.2 us (3%)
    reduce_scatter x1, waiting for transfers between devices, shards(): lax.psum_scatter(returned, 'tensor', scatter_dimension=1, tiled=True)  110 us
    all_to_all x1, blocking collectives, shards(): lax.all_to_all(partial_out, 'batch', split_axis=0, concat_axis=1, tiled=T...  74.2 us
    all_gather x1, waiting for transfers between devices, shards(): whole_rows = lax.all_gather(stream, 'tensor', axis=1, tiled=True)  64.9 us
    unnamed x14, local copies, waits for them, and re-layouts  51.6 us
    reshape x1, local copies, waits for them, and re-layouts, shards(): fc1_weight.reshape(width_part, local_blocks, BLOCK)  48.6 us
    reduce_scatter x1, waiting for transfers between devices, shards(): lax.psum_scatter(partial_value, 'batch', scatter_dimension=0, tiled=True)  13.4 us
    gather x1, local copies, waits for them, and re-layouts, shards(): jnp.take(fc2_weight.reshape(local_blocks, BLOCK, down_width), slot_block,...  10.3 us
    gather x1, local copies, waits for them, and re-layouts, shards(): jnp.take(fc1_weight.reshape(width_part, local_blocks, BLOCK), slot_block,...  9.86 us
  transfers between devices with their start and end apart: 4, of which 3 were waited for; matrix products, arithmetic and copies ran while one was open for 27% of the time, Pallas kernels for 0%

commit v1 on v0

v1 whole, which is shorter than its diff:
```python
import functools

import jax
import jax.numpy as jnp
from jax import lax
from jax.experimental import pallas as pl
from jax.experimental.pallas import tpu as pltpu
from jax.sharding import PartitionSpec as P

BLOCK = 128
CAP = 4
PIECES = 2
VMEM_LIMIT = 40 * 1024 * 1024
bf16 = jnp.bfloat16
f32 = jnp.float32

VMEM = pl.BlockSpec(memory_space=pltpu.VMEM)
SMEM = pl.BlockSpec(memory_space=pltpu.SMEM)
ANY = pl.BlockSpec(memory_space=pl.ANY)


def call(body, outs, in_specs, out_specs=None, scratch=(), flops=0, moved=0, aliases=None, grid=()):
    return pl.pallas_call(
        body,
        grid=grid,
        out_shape=outs,
        in_specs=in_specs,
        out_specs=out_specs if out_specs is not None else jax.tree.map(lambda _: VMEM, outs),
        scratch_shapes=list(scratch),
        input_output_aliases=aliases or {},
        compiler_params=pltpu.CompilerParams(vmem_limit_bytes=VMEM_LIMIT),
        cost_estimate=pl.CostEstimate(flops=flops, bytes_accessed=moved, transcendentals=0),
    )


def slots(active_ids, active_counts, local_blocks, tensor_index):
    slot_total = active_ids.shape[1]
    local_ids = active_ids - tensor_index * local_blocks
    present = (
        (jnp.arange(slot_total)[None, :] < active_counts[:, None])
        & (local_ids >= 0)
        & (local_ids < local_blocks)
    )
    present_int = present.astype(jnp.int32)
    position = jnp.cumsum(present_int, axis=1) - 1
    matches = present_int[:, :, None] * (
        position[:, :, None] == jnp.arange(CAP)[None, None, :]
    ).astype(jnp.int32)
    slot_block = jnp.sum(matches * local_ids[:, :, None], axis=1)
    live_total = jnp.sum(present_int, axis=1)
    return slot_block, live_total


def norm_kernel(where_ref, own, near, far, mid, fwd, gain, shift, *rest):
    outs, scr = rest[:4], rest[4]
    rows, width = own.shape
    step = 16
    t, s = where_ref[0], where_ref[1]
    full = 4 * width

    def chunk(i, _):
        at = pl.ds(pl.multiple_of(i * step, step), step)

        def part(k):
            if k == 0:
                return own[at, :].astype(f32)
            if k == 1:
                return near[at, :].astype(f32)
            if k == 2:
                return far[at, :].astype(f32)
            return mid[at, :].astype(f32) + fwd[at, :].astype(f32)

        total = sum(jnp.sum(part(k), axis=1, keepdims=True) for k in range(4))
        center = total / full
        square = sum(
            jnp.sum(jnp.square(part(k) - center), axis=1, keepdims=True) for k in range(4)
        )
        factor = lax.rsqrt(square / full + 1e-05)
        for k in range(4):
            f = jnp.bitwise_xor(t, k)
            scaled = (part(k) - center) * factor
            scr[jnp.bitwise_xor(s, k), at, :] = (scaled * gain[f] + shift[f]).astype(bf16)
        return 0

    lax.fori_loop(0, rows // step, chunk, 0)
    for j in range(4):
        outs[j][...] = scr[j]


def normalize(where, own, near, far, mid, fwd, gain, shift):
    shape = own.shape
    out = jax.ShapeDtypeStruct(shape, bf16)
    return call(
        norm_kernel,
        [out] * 4,
        [SMEM] + [VMEM] * 7,
        scratch=[pltpu.VMEM((4,) + shape, bf16)],
        flops=4 * shape[0] * shape[1] * 12,
        moved=shape[0] * shape[1] * 2 * 9,
    )(where, own, near, far, mid, fwd, gain, shift)


def up_kernel(parts, sid, live, *refs):
    n = len(parts)
    xs, w, outs, buf, sems = refs[:n], refs[n], refs[n + 1 : 2 * n + 1], refs[2 * n + 1], refs[2 * n + 2]

    def copies(q):
        j = parts[q]
        for k in range(CAP):
            at = pl.ds(pl.multiple_of(sid[j, k] * BLOCK, BLOCK), BLOCK)
            yield k < live[j], pltpu.make_async_copy(
                w.at[:, at], buf.at[q, :, pl.ds(k * BLOCK, BLOCK)], sems.at[q, k]
            )

    for q in range(n):
        for on, copy in copies(q):
            pl.when(on)(copy.start)
    for q in range(n):
        for on, copy in copies(q):
            pl.when(on)(copy.wait)
        outs[q][...] = jnp.dot(xs[q][...], buf[q], preferred_element_type=f32).astype(outs[q].dtype)


def up(parts, kinds, sid, live, xs, w):
    n = len(parts)
    rows, width = xs[0].shape
    return call(
        functools.partial(up_kernel, parts),
        [jax.ShapeDtypeStruct((rows, CAP * BLOCK), kind) for kind in kinds],
        [SMEM, SMEM] + [VMEM] * n + [ANY],
        scratch=[pltpu.VMEM((n, width, CAP * BLOCK), bf16), pltpu.SemaphoreType.DMA((n, CAP))],
        flops=n * rows * width * CAP * BLOCK * 2,
        moved=n * width * CAP * BLOCK * 2,
    )(sid, live, *xs, w)


def down_kernel(parts, sid, live, *refs):
    n = len(parts)
    hs, w, outs, buf, sems = refs[:n], refs[n], refs[n + 1 : 2 * n + 1], refs[2 * n + 1], refs[2 * n + 2]

    def copies(q):
        j = parts[q]
        for k in range(CAP):
            at = pl.ds(pl.multiple_of(sid[j, k] * BLOCK, BLOCK), BLOCK)
            yield k < live[j], pltpu.make_async_copy(
                w.at[at, :], buf.at[q, pl.ds(k * BLOCK, BLOCK), :], sems.at[q, k]
            )

    for q in range(n):
        for k, (on, copy) in enumerate(copies(q)):
            pl.when(on)(copy.start)

            @pl.when(jnp.logical_not(on))
            def _():
                buf[q, pl.ds(k * BLOCK, BLOCK), :] = jnp.zeros((BLOCK, buf.shape[2]), bf16)

    for q in range(n):
        for on, copy in copies(q):
            pl.when(on)(copy.wait)
        outs[q][...] = jnp.dot(hs[q][...], buf[q], preferred_element_type=f32).astype(outs[q].dtype)


def down(parts, sid, live, hs, w):
    n = len(parts)
    rows = hs[0].shape[0]
    width = w.shape[1]
    return call(
        functools.partial(down_kernel, parts),
        [jax.ShapeDtypeStruct((rows, width), bf16)] * n,
        [SMEM, SMEM] + [VMEM] * n + [ANY],
        scratch=[pltpu.VMEM((n, CAP * BLOCK, width), bf16), pltpu.SemaphoreType.DMA((n, CAP))],
        flops=n * rows * width * CAP * BLOCK * 2,
        moved=n * width * CAP * BLOCK * 2,
    )(sid, live, *hs, w)


def pair_kernel(p0, p2, r1, r3, s_ref, send):
    rows = p0.shape[0]
    for i, (p, r) in enumerate(((p0, r1), (p2, r3))):
        total = p[...] + r[...].astype(f32)
        at = pl.ds(i * rows, rows)
        s_ref[at, :] = total
        send[at, :] = total.astype(bf16)


def hidden_kernel(live, s_ref, got, bias, out):
    rows = s_ref.shape[0] // 2
    lane = lax.broadcasted_iota(jnp.int32, (rows, CAP * BLOCK), 1)
    for i in range(2):
        at, other = pl.ds(i * rows, rows), pl.ds((1 - i) * rows, rows)
        value = s_ref[at, :] + got[other, :].astype(f32) + bias[i]
        on = lane < live[2 * i] * BLOCK
        out[at, :] = jnp.where(on, jnp.maximum(value, 0.0), 0.0).astype(bf16)


def route_kernel(where_ref, y0, y1, y2, y3, z0, z1, z2, z3, scr):
    s = where_ref[1]
    for j, y in enumerate((y0, y1, y2, y3)):
        scr[jnp.bitwise_xor(s, j)] = y[...]
    for k, z in enumerate((z0, z1, z2, z3)):
        z[...] = scr[k]


def final_kernel(x, z0, k1, mid, k2, bias, *refs):
    out = refs[-1]
    total = x[...].astype(f32) + z0[...].astype(f32) + k1[...].astype(f32)
    total = total + (mid[...].astype(f32) + k2[...].astype(f32)) + bias[...]
    out[...] = total.astype(bf16)


def swap(x, axis, pairs):
    return lax.ppermute(x, axis, pairs)


NEAR = [(0, 1), (1, 0), (2, 3), (3, 2)]
FAR = [(0, 2), (2, 0), (1, 3), (3, 1)]
CROSS = [(0, 3), (3, 0), (1, 2), (2, 1)]
MIDDLE = [(1, 2), (2, 1)]
OUTWARD = [(1, 0), (2, 3)]
INWARD = [(0, 1), (3, 2)]
BATCH = {1: NEAR, 2: FAR, 3: CROSS}


def small_mesh(
    stream, ln_gain, ln_bias, fc1_weight, fc1_bias, fc2_weight, fc2_bias, active_ids, active_counts
):
    t = lax.axis_index("tensor")
    b = lax.axis_index("batch")
    rows, width = stream.shape
    local_blocks = fc1_weight.shape[1] // BLOCK
    m = rows // PIECES

    slot_block, live_total = slots(active_ids, active_counts, local_blocks, t)
    order = jnp.bitwise_xor(b, jnp.arange(4))
    sid = jnp.take(slot_block, order, axis=0)
    live = jnp.take(live_total, order, axis=0)
    bias_table = fc1_bias.reshape(local_blocks, BLOCK).astype(f32)
    up_bias = jnp.take(bias_table, sid[::2], axis=0).reshape(2, 1, CAP * BLOCK)
    where = jnp.stack([t, jnp.bitwise_xor(t, b)]).astype(jnp.int32)
    gain = ln_gain.astype(f32).reshape(4, 1, width)
    shift = ln_bias.astype(f32).reshape(4, 1, width)
    down_bias = fc2_bias.astype(f32).reshape(1, width)

    out = None
    for p in range(PIECES):
        x = stream[p * m : (p + 1) * m]
        far = swap(x, "tensor", FAR)
        near = swap(x, "tensor", NEAR)
        mid = swap(x, "tensor", MIDDLE)
        fwd = swap(far, "tensor", OUTWARD)
        n = normalize(where, x, near, far, mid, fwd, gain, shift)
        n = [n[0]] + [swap(n[j], "batch", BATCH[j]) for j in (1, 2, 3)]
        p0, p1 = up((0, 1), (f32, bf16), sid, live, n[:2], fc1_weight)
        p2, p3 = up((2, 3), (f32, bf16), sid, live, n[2:], fc1_weight)
        r1 = swap(p1, "batch", NEAR)
        r3 = swap(p3, "batch", NEAR)
        total = (2 * m, CAP * BLOCK)
        s_mine, s_send = call(
            pair_kernel,
            [jax.ShapeDtypeStruct(total, f32), jax.ShapeDtypeStruct(total, bf16)],
            [VMEM] * 4,
        )(p0, p2, r1, r3)
        got = swap(s_send, "batch", FAR)
        mine = call(
            hidden_kernel, jax.ShapeDtypeStruct(total, bf16), [SMEM] + [VMEM] * 3, VMEM
        )(live, s_mine, got, up_bias)
        other = swap(mine, "batch", NEAR)
        y2, y3 = down((2, 3), sid, live, [mine[m:], other[m:]], fc2_weight)
        y0, y1 = down((0, 1), sid, live, [mine[:m], other[:m]], fc2_weight)
        y1, y2, y3 = [swap(y, "batch", BATCH[j]) for j, y in ((1, y1), (2, y2), (3, y3))]
        part = jax.ShapeDtypeStruct((m, width), bf16)
        z0, z1, z2, z3 = call(
            route_kernel,
            [part] * 4,
            [SMEM] + [VMEM] * 4,
            scratch=[pltpu.VMEM((4, m, width), bf16)],
        )(where, y0, y1, y2, y3)
        mid = swap(z3, "tensor", MIDDLE)
        fwd = swap(z3, "tensor", INWARD)
        k1 = swap(z1, "tensor", NEAR)
        k2 = swap((z2.astype(f32) + fwd.astype(f32)).astype(bf16), "tensor", FAR)
        args = [x, z0, k1, mid, k2, down_bias]
        specs = [VMEM] * 6
        aliases = {}
        if out is not None:
            args.append(out)
            specs.append(ANY)
            aliases = {6: 0}
        out = call(
            final_kernel,
            jax.ShapeDtypeStruct((rows, width), bf16),
            specs,
            pl.BlockSpec((m, width), functools.partial(lambda p, i: (p, 0), p)),
            aliases=aliases,
            grid=(1,),
        )(*args)
    return out


def any_mesh(
    stream, ln_gain, ln_bias, fc1_weight, fc1_bias, fc2_weight, fc2_bias, active_ids, active_counts
):
    batches = lax.axis_size("batch")
    whole_rows = lax.all_gather(stream, "tensor", axis=1, tiled=True)
    values = whole_rows.astype(f32)
    center = jnp.mean(values, axis=-1, keepdims=True)
    spread = jnp.mean(jnp.square(values - center), axis=-1, keepdims=True)
    scaled = (values - center) * lax.rsqrt(spread + 1e-05)
    normed = (scaled * ln_gain.astype(f32) + ln_bias.astype(f32)).astype(bf16)
    columns = lax.all_to_all(normed, "batch", split_axis=1, concat_axis=0, tiled=True)
    rows = stream.shape[0]
    width = columns.shape[1]
    local_blocks = fc1_weight.shape[1] // BLOCK
    sid, live = slots(active_ids, active_counts, local_blocks, lax.axis_index("tensor"))
    bias_table = fc1_bias.reshape(local_blocks, BLOCK).astype(f32)
    bias = jnp.take(bias_table, sid, axis=0).reshape(batches, 1, CAP * BLOCK)
    on = jnp.arange(CAP * BLOCK)[None, None, :] < live[:, None, None] * BLOCK
    parts = []
    for r in range(batches):
        parts += up((r,), (f32,), sid, live, [columns[r * rows : (r + 1) * rows]], fc1_weight)
    share = lax.psum_scatter(jnp.stack(parts), "batch", scatter_dimension=0, tiled=True)
    index = lax.axis_index("batch")
    my_bias = lax.dynamic_slice_in_dim(bias, index, 1, 0)
    my_on = lax.dynamic_slice_in_dim(on, index, 1, 0)
    mine = jnp.where(my_on, jnp.maximum(share + my_bias, 0.0), 0.0).astype(bf16)
    hidden = lax.all_gather(mine, "batch", axis=0, tiled=True)
    outs = []
    for r in range(batches):
        outs += down((r,), sid, live, [hidden[r]], fc2_weight)
    returned = lax.all_to_all(
        jnp.concatenate(outs), "batch", split_axis=0, concat_axis=1, tiled=True
    )
    summed = lax.psum_scatter(returned.astype(f32), "tensor", scatter_dimension=1, tiled=True)
    return (stream.astype(f32) + summed + fc2_bias.astype(f32)).astype(bf16)


def solution(mesh):
    in_specs = (
        P(("groups", "batch"), "tensor"),
        P(),
        P(),
        P("batch", "tensor"),
        P("tensor"),
        P("tensor", "batch"),
        P("tensor"),
        P("groups", None),
        P("groups"),
    )
    out_specs = P(("groups", "batch"), "tensor")
    body = small_mesh if mesh.shape["tensor"] == 4 and mesh.shape["batch"] == 4 else any_mesh
    return jax.shard_map(body, mesh=mesh, in_specs=in_specs, out_specs=out_specs, check_vma=False)
```

time: 453 us -> 207 us (0.46)
  local copies, waits for them, and re-layouts: 132 us -> 4.82 us
  blocking collectives: 81 us -> 0 us
  waiting for transfers between devices: 189 us -> 109 us
  Pallas kernels: 0 us -> 43.4 us
  starting transfers between devices: 3.78 us -> 45.5 us
  other arithmetic: 17.9 us -> 3.87 us
  matrix products: 13.8 us -> 0 us
  between operations: 13.2 us -> 0.4 us
    reduce_scatter x2 -> x0, waiting for transfers between devices: 124 us -> none  [the longest x1 110 us: shards(): lax.psum_scatter(returned, 'tensor', scatter_dimension=1, tiled=True)]
    ppermute x0 -> x36, waiting for transfers between devices: none -> 109 us  [swap(): return lax.ppermute(x, axis, pairs)]
    all_to_all x1 -> x0, blocking collectives: 74.2 us -> none  [shards(): lax.all_to_all(partial_out, 'batch', split_axis=0, concat_axis=1, tiled=T...]
    all_gather x1 -> x0, waiting for transfers between devices: 64.9 us -> none  [shards(): whole_rows = lax.all_gather(stream, 'tensor', axis=1, tiled=True)]
    unnamed x14 -> x6, local copies, waits for them, and re-layouts: 51.6 us -> 1.74 us
    reshape x1 -> x0, local copies, waits for them, and re-layouts: 48.6 us -> none  [shards(): fc1_weight.reshape(width_part, local_blocks, BLOCK)]
    ppermute x0 -> x36, starting transfers between devices: none -> 45.5 us  [swap(): return lax.ppermute(x, axis, pairs)]
    pallas_call x0 -> x18, Pallas kernels: none -> 43.4 us  [the longest x4 16.3 us: up(): call(functools.partial(up_kernel, parts), [jax.ShapeDtypeStruct((rows, CA...]
  transfers between devices with their start and end apart: 4 -> 36, of which waited for: 3 -> 16; matrix products, arithmetic and copies ran while one was open for 27% -> 3% of each run, Pallas kernels for 0% -> 20%
where the time goes in v1:
time: 207 us
  waiting for transfers between devices  109 us (53%)
  starting transfers between devices  45.5 us (22%)
  Pallas kernels  43.4 us (21%)
  local copies, waits for them, and re-layouts  4.82 us (2%)
  other arithmetic  3.87 us (2%)
    ppermute x36, waiting for transfers between devices, swap(): return lax.ppermute(x, axis, pairs)  109 us
    ppermute x36, starting transfers between devices, swap(): return lax.ppermute(x, axis, pairs)  45.5 us
    pallas_call x4, Pallas kernels, up(): call(functools.partial(up_kernel, parts), [jax.ShapeDtypeStruct((rows, CA...  16.3 us
    pallas_call x4, Pallas kernels, down(): call(functools.partial(down_kernel, parts), [jax.ShapeDtypeStruct((rows,...  15.3 us
    pallas_call x2, Pallas kernels, normalize(): call(norm_kernel, [out] * 4, [SMEM] + [VMEM] * 7, scratch=[pltpu.VMEM((4,...  6.94 us
  transfers between devices with their start and end apart: 36, of which 16 were waited for; matrix products, arithmetic and copies ran while one was open for 3% of the time, Pallas kernels for 20%

profile of v1, /device:TPU:0, one launch (start us, length us, event | category | flops | bytes accessed | tf_op | source)
XLA Modules:
  0.0 206.5 jit_solution(2442072260404102918)
XLA Ops:
  0.0 1.2 fusion.6
  1.2 4.1 %collective-permute-start.19 = (bf16[64,3072]{1,0:T(8,128)(2,1)S(1)}, bf16[64,3072]{1,0:T(8,128)(2,1)S(1)}, u32[]{:S(2)}, u32[]{:S(2)}) collective-permute-start(bf16[64,3072]{1,0:T(8,128)(2,1)S(1)} %get-tuple-element.80.own.x), channel_id=1, source_target_pairs={{0,8},{8,0},{4,12},{12,4},{1,9},{9,1},{5,13},{13,5},{2,10},{10,2},... | collective-permute-start | bytes 1179656 | tf_op jit(solution)/shard_map/ppermute | solution.py:212
  5.3 1.6 collective-permute-start.18
  7.5 3.2 %collective-permute-start.1 = (bf16[64,3072]{1,0:T(8,128)(2,1)S(1)}, bf16[64,3072]{1,0:T(8,128)(2,1)S(1)}, u32[]{:S(2)}, u32[]{:S(2)}) collective-permute-start(bf16[64,3072]{1,0:T(8,128)(2,1)S(1)} %get-tuple-element.81.own.x), channel_id=1, source_target_pairs={{0,8},{8,0},{4,12},{12,4},{1,9},{9,1},{5,13},{13,5},{2,10},{10,2},... | collective-permute-start | bytes 1179656 | tf_op jit(solution)/shard_map/ppermute | solution.py:212
  10.7 0.7 reshape.82
  12.2 0.9 fusion.4
  14.7 9.9 %collective-permute-done.19.far = bf16[64,3072]{1,0:T(8,128)(2,1)S(1)} collective-permute-done((bf16[64,3072]{1,0:T(8,128)(2,1)S(1)}, bf16[64,3072]{1,0:T(8,128)(2,1)S(1)}, u32[]{:S(2)}, u32[]{:S(2)}) %collective-permute-start.19) | collective-permute-done | bytes 393248 | tf_op jit(solution)/shard_map/ppermute | solution.py:212
  24.6 1.3 collective-permute-start.21
  26.7 22.3 %collective-permute-done.1.far = bf16[64,3072]{1,0:T(8,128)(2,1)S(1)} collective-permute-done((bf16[64,3072]{1,0:T(8,128)(2,1)S(1)}, bf16[64,3072]{1,0:T(8,128)(2,1)S(1)}, u32[]{:S(2)}, u32[]{:S(2)}) %collective-permute-start.1) | collective-permute-done | bytes 393248 | tf_op jit(solution)/shard_map/ppermute | solution.py:212
  49.0 1.3 collective-permute-start.3
  51.1 1.0 copy-done.1
  52.1 3.4 %shard_map.99 = (bf16[64,3072]{1,0:T(8,128)(2,1)S(1)}, bf16[64,3072]{1,0:T(8,128)(2,1)}, bf16[64,3072]{1,0:T(8,128)(2,1)S(1)}, bf16[64,3072]{1,0:T(8,128)(2,1)}) custom-call(s32[2]{0:T(128)S(1)} %pad_add_fusion.where_ref, bf16[64,3072]{1,0:T(8,128)(2,1)S(1)} %get-tuple-element.80.own.x, bf16[64,3072]{1,0:T(8,128)(2,1)S(1)} %collective-permute-done.18.near, ...), custom_call_target="tpu_custom_call" | custom-call | flops 9437184 | bytes 3538944 | tf_op jit(solution)/shard_map/pallas_call | solution.py:93
  55.5 1.8 collective-permute-start.23
  57.7 2.7 %collective-permute-done.3.fwd = bf16[64,3072]{1,0:T(8,128)(2,1)S(1)} collective-permute-done((bf16[64,3072]{1,0:T(8,128)(2,1)S(1)}, bf16[64,3072]{1,0:T(8,128)(2,1)S(1)}, u32[]{:S(2)}, u32[]{:S(2)}) %collective-permute-start.3) | collective-permute-done | bytes 393248 | tf_op jit(solution)/shard_map/ppermute | solution.py:212
  60.4 3.5 %shard_map.91 = (bf16[64,3072]{1,0:T(8,128)(2,1)S(1)}, bf16[64,3072]{1,0:T(8,128)(2,1)}, bf16[64,3072]{1,0:T(8,128)(2,1)}, bf16[64,3072]{1,0:T(8,128)(2,1)}) custom-call(s32[2]{0:T(128)S(1)} %pad_add_fusion.where_ref, bf16[64,3072]{1,0:T(8,128)(2,1)S(1)} %get-tuple-element.81.own.x, bf16[64,3072]{1,0:T(8,128)(2,1)S(1)} %collective-permute-done.near, ...), custom_call_target="tpu_custom_call" | custom-call | flops 9437184 | bytes 3538944 | tf_op jit(solution)/shard_map/pallas_call | solution.py:93
  63.9 1.2 collective-permute-start.5
  65.2 2.4 %collective-permute-done.23.refs_0_ = bf16[64,3072]{1,0:T(8,128)(2,1)S(1)} collective-permute-done((bf16[64,3072]{1,0:T(8,128)(2,1)S(1)}, bf16[64,3072]{1,0:T(8,128)(2,1)S(1)}, u32[]{:S(2)}, u32[]{:S(2)}) %collective-permute-start.23) | collective-permute-done | bytes 393248 | tf_op jit(solution)/shard_map/ppermute | solution.py:212
  68.3 7.1 %collective-permute-done.24.refs_1_ = bf16[64,3072]{1,0:T(8,128)(2,1)} collective-permute-done((bf16[64,3072]{1,0:T(8,128)(2,1)}, bf16[64,3072]{1,0:T(8,128)(2,1)}, u32[]{:S(2)}, u32[]{:S(2)}) %collective-permute-start.24) | collective-permute-done | bytes 393248 | tf_op jit(solution)/shard_map/ppermute | solution.py:212
  75.4 4.3 %shard_map.101 = (f32[64,512]{1,0:T(8,128)S(1)}, bf16[64,512]{1,0:T(8,128)(2,1)S(1)}) custom-call(s32[4,4]{1,0:T(4,128)S(1)} %broadcast_select_fusion.1.sid, s32[4]{0:T(128)S(1)} %broadcast_select_fusion.2.live, bf16[64,3072]{1,0:T(8,128)(2,1)S(1)} %collective-permute-done.23.refs_0_, bf16[64,3072]{1,0:T(8,128)(2,1)} %collective-permute-done.24.refs_1_, ...), custom_call_target="tpu_custom_call" | custom-call | flops 402653184 | bytes 6291456 | tf_op jit(solution)/shard_map/pallas_call | solution.py:127
  79.8 3.9 %shard_map.100 = (f32[64,512]{1,0:T(8,128)S(1)}, bf16[64,512]{1,0:T(8,128)(2,1)S(1)}) custom-call(s32[4,4]{1,0:T(4,128)S(1)} %broadcast_select_fusion.1.sid, s32[4]{0:T(128)S(1)} %broadcast_select_fusion.2.live, bf16[64,3072]{1,0:T(8,128)(2,1)S(1)} %get-tuple-element.59.refs_0_, bf16[64,3072]{1,0:T(8,128)(2,1)S(1)} %collective-permute-done.22.refs_1_, ...), custom_call_target="tpu_custom_call" | custom-call | flops 402653184 | bytes 6291456 | tf_op jit(solution)/shard_map/pallas_call | solution.py:127
  84.4 4.7 %collective-permute-done.6.refs_1_ = bf16[64,3072]{1,0:T(8,128)(2,1)} collective-permute-done((bf16[64,3072]{1,0:T(8,128)(2,1)}, bf16[64,3072]{1,0:T(8,128)(2,1)}, u32[]{:S(2)}, u32[]{:S(2)}) %collective-permute-start.6) | collective-permute-done | bytes 393248 | tf_op jit(solution)/shard_map/ppermute | solution.py:212
  89.1 4.3 %shard_map.93 = (f32[64,512]{1,0:T(8,128)S(1)}, bf16[64,512]{1,0:T(8,128)(2,1)S(1)}) custom-call(s32[4,4]{1,0:T(4,128)S(1)} %broadcast_select_fusion.1.sid, s32[4]{0:T(128)S(1)} %broadcast_select_fusion.2.live, bf16[64,3072]{1,0:T(8,128)(2,1)S(1)} %collective-permute-done.5.refs_0_, bf16[64,3072]{1,0:T(8,128)(2,1)} %collective-permute-done.6.refs_1_, ...), custom_call_target="tpu_custom_call" | custom-call | flops 402653184 | bytes 6291456 | tf_op jit(solution)/shard_map/pallas_call | solution.py:127
  93.9 3.9 %shard_map.92 = (f32[64,512]{1,0:T(8,128)S(1)}, bf16[64,512]{1,0:T(8,128)(2,1)S(1)}) custom-call(s32[4,4]{1,0:T(4,128)S(1)} %broadcast_select_fusion.1.sid, s32[4]{0:T(128)S(1)} %broadcast_select_fusion.2.live, bf16[64,3072]{1,0:T(8,128)(2,1)S(1)} %get-tuple-element.41.refs_0_, bf16[64,3072]{1,0:T(8,128)(2,1)S(1)} %collective-permute-done.4.refs_1_, ...), custom_call_target="tpu_custom_call" | custom-call | flops 402653184 | bytes 6291456 | tf_op jit(solution)/shard_map/pallas_call | solution.py:127
  98.4 1.3 collective-permute-start.27
  99.8 0.8 collective-permute-start.9
  100.7 4.1 %collective-permute-done.27.got = bf16[128,512]{1,0:T(8,128)(2,1)S(1)} collective-permute-done((bf16[128,512]{1,0:T(8,128)(2,1)S(1)}, bf16[128,512]{1,0:T(8,128)(2,1)S(1)}, u32[]{:S(2)}, u32[]{:S(2)}) %collective-permute-start.27) | collective-permute-done | bytes 131104 | tf_op jit(solution)/shard_map/ppermute | solution.py:212
  105.5 1.7 collective-permute-done.9.got
  107.9 3.8 %shard_map.105 = (bf16[64,3072]{1,0:T(8,128)(2,1)S(1)}, bf16[64,3072]{1,0:T(8,128)(2,1)S(1)}) custom-call(s32[4,4]{1,0:T(4,128)S(1)} %broadcast_select_fusion.1.sid, s32[4]{0:T(128)S(1)} %broadcast_select_fusion.2.live, bf16[64,512]{1,0:T(8,128)(2,1)S(1)} %get-tuple-element.84.refs_0_, bf16[64,512]{1,0:T(8,128)(2,1)S(1)} %get-tuple-element.82.refs_1_, ...), custom_call_target="tpu_custom_call" | custom-call | flops 402653184 | bytes 6291456 | tf_op jit(solution)/shard_map/pallas_call | solution.py:167
  111.8 1.3 collective-permute-start.30
  113.2 3.8 %shard_map.104 = (bf16[64,3072]{1,0:T(8,128)(2,1)S(1)}, bf16[64,3072]{1,0:T(8,128)(2,1)S(1)}) custom-call(s32[4,4]{1,0:T(4,128)S(1)} %broadcast_select_fusion.1.sid, s32[4]{0:T(128)S(1)} %broadcast_select_fusion.2.live, bf16[64,512]{1,0:T(8,128)(2,1)S(1)} %get-tuple-element.85.refs_0_, bf16[64,512]{1,0:T(8,128)(2,1)S(1)} %get-tuple-element.83.refs_1_, ...), custom_call_target="tpu_custom_call" | custom-call | flops 402653184 | bytes 6291456 | tf_op jit(solution)/shard_map/pallas_call | solution.py:167
  117.5 3.8 %shard_map.97 = (bf16[64,3072]{1,0:T(8,128)(2,1)S(1)}, bf16[64,3072]{1,0:T(8,128)(2,1)S(1)}) custom-call(s32[4,4]{1,0:T(4,128)S(1)} %broadcast_select_fusion.1.sid, s32[4]{0:T(128)S(1)} %broadcast_select_fusion.2.live, bf16[64,512]{1,0:T(8,128)(2,1)S(1)} %get-tuple-element.88.refs_0_, bf16[64,512]{1,0:T(8,128)(2,1)S(1)} %get-tuple-element.86.refs_1_, ...), custom_call_target="tpu_custom_call" | custom-call | flops 402653184 | bytes 6291456 | tf_op jit(solution)/shard_map/pallas_call | solution.py:167
  121.3 1.3 collective-permute-start.12
  122.6 3.8 %shard_map.96 = (bf16[64,3072]{1,0:T(8,128)(2,1)S(1)}, bf16[64,3072]{1,0:T(8,128)(2,1)S(1)}) custom-call(s32[4,4]{1,0:T(4,128)S(1)} %broadcast_select_fusion.1.sid, s32[4]{0:T(128)S(1)} %broadcast_select_fusion.2.live, bf16[64,512]{1,0:T(8,128)(2,1)S(1)} %get-tuple-element.89.refs_0_, bf16[64,512]{1,0:T(8,128)(2,1)S(1)} %get-tuple-element.87.refs_1_, ...), custom_call_target="tpu_custom_call" | custom-call | flops 402653184 | bytes 6291456 | tf_op jit(solution)/shard_map/pallas_call | solution.py:167
  127.0 4.0 %collective-permute-done.31.y3 = bf16[64,3072]{1,0:T(8,128)(2,1)S(1)} collective-permute-done((bf16[64,3072]{1,0:T(8,128)(2,1)S(1)}, bf16[64,3072]{1,0:T(8,128)(2,1)S(1)}, u32[]{:S(2)}, u32[]{:S(2)}) %collective-permute-start.31) | collective-permute-done | bytes 393248 | tf_op jit(solution)/shard_map/ppermute | solution.py:212
  131.0 0.7 shard_map.106
  131.8 5.1 %collective-permute-start.34 = (bf16[64,3072]{1,0:T(8,128)(2,1)S(1)}, bf16[64,3072]{1,0:T(8,128)(2,1)S(1)}, u32[]{:S(2)}, u32[]{:S(2)}) collective-permute-start(bf16[64,3072]{1,0:T(8,128)(2,1)S(1)} %get-tuple-element.75), channel_id=1, source_target_pairs={{0,4},{12,8},{1,5},{13,9},{2,6},{14,10},{3,7},{15,11},{16,20},{28,... | collective-permute-start | bytes 1179656 | tf_op jit(solution)/shard_map/ppermute | solution.py:212
  137.5 3.1 %collective-permute-done.12.y2 = bf16[64,3072]{1,0:T(8,128)(2,1)S(1)} collective-permute-done((bf16[64,3072]{1,0:T(8,128)(2,1)S(1)}, bf16[64,3072]{1,0:T(8,128)(2,1)S(1)}, u32[]{:S(2)}, u32[]{:S(2)}) %collective-permute-start.12) | collective-permute-done | bytes 393248 | tf_op jit(solution)/shard_map/ppermute | solution.py:212
  140.7 6.6 %collective-permute-done.13.y3 = bf16[64,3072]{1,0:T(8,128)(2,1)S(1)} collective-permute-done((bf16[64,3072]{1,0:T(8,128)(2,1)S(1)}, bf16[64,3072]{1,0:T(8,128)(2,1)S(1)}, u32[]{:S(2)}, u32[]{:S(2)}) %collective-permute-start.13) | collective-permute-done | bytes 393248 | tf_op jit(solution)/shard_map/ppermute | solution.py:212
  147.3 0.7 shard_map.98
  148.0 5.7 %collective-permute-start.16 = (bf16[64,3072]{1,0:T(8,128)(2,1)S(1)}, bf16[64,3072]{1,0:T(8,128)(2,1)S(1)}, u32[]{:S(2)}, u32[]{:S(2)}) collective-permute-start(bf16[64,3072]{1,0:T(8,128)(2,1)S(1)} %get-tuple-element.57), channel_id=1, source_target_pairs={{0,4},{12,8},{1,5},{13,9},{2,6},{14,10},{3,7},{15,11},{16,20},{28,... | collective-permute-start | bytes 1179656 | tf_op jit(solution)/shard_map/ppermute | solution.py:212
  154.4 4.5 %collective-permute-start.32 = (bf16[64,3072]{1,0:T(8,128)(2,1)S(1)}, bf16[64,3072]{1,0:T(8,128)(2,1)S(1)}, u32[]{:S(2)}, u32[]{:S(2)}) collective-permute-start(bf16[64,3072]{1,0:T(8,128)(2,1)S(1)} %get-tuple-element.74), channel_id=1, source_target_pairs={{0,4},{4,0},{8,12},{12,8},{1,5},{5,1},{9,13},{13,9},{2,6},{6,2},{1... | collective-permute-start | bytes 1179656 | tf_op jit(solution)/shard_map/ppermute | solution.py:212
  159.0 4.1 %collective-permute-done.16 = bf16[64,3072]{1,0:T(8,128)(2,1)S(1)} collective-permute-done((bf16[64,3072]{1,0:T(8,128)(2,1)S(1)}, bf16[64,3072]{1,0:T(8,128)(2,1)S(1)}, u32[]{:S(2)}, u32[]{:S(2)}) %collective-permute-start.16) | collective-permute-done | bytes 393248 | tf_op jit(solution)/shard_map/ppermute | solution.py:212
  163.1 5.7 %collective-permute-start.35 = (bf16[64,3072]{1,0:T(8,128)(2,1)S(1)}, bf16[64,3072]{1,0:T(8,128)(2,1)S(1)}, u32[]{:S(2)}, u32[]{:S(2)}) collective-permute-start(bf16[64,3072]{1,0:T(8,128)(2,1)S(1)} %add_convert_fusion), channel_id=1, source_target_pairs={{0,8},{8,0},{4,12},{12,4},{1,9},{9,1},{5,13},{13,5},{2,10},{10,2},... | collective-permute-start | bytes 1179656 | tf_op jit(solution)/shard_map/ppermute | solution.py:212
  168.9 12.5 %collective-permute-done.32.k1 = bf16[64,3072]{1,0:T(8,128)(2,1)S(1)} collective-permute-done((bf16[64,3072]{1,0:T(8,128)(2,1)S(1)}, bf16[64,3072]{1,0:T(8,128)(2,1)S(1)}, u32[]{:S(2)}, u32[]{:S(2)}) %collective-permute-start.32) | collective-permute-done | bytes 393248 | tf_op jit(solution)/shard_map/ppermute | solution.py:212
  181.7 6.7 %collective-permute-done.35.k2 = bf16[64,3072]{1,0:T(8,128)(2,1)S(1)} collective-permute-done((bf16[64,3072]{1,0:T(8,128)(2,1)S(1)}, bf16[64,3072]{1,0:T(8,128)(2,1)S(1)}, u32[]{:S(2)}, u32[]{:S(2)}) %collective-permute-start.35) | collective-permute-done | bytes 393248 | tf_op jit(solution)/shard_map/ppermute | solution.py:212
  188.4 1.0 shard_map.107.refs_0_
  189.5 16.0 %collective-permute-done.17.k2 = bf16[64,3072]{1,0:T(8,128)(2,1)S(1)} collective-permute-done((bf16[64,3072]{1,0:T(8,128)(2,1)S(1)}, bf16[64,3072]{1,0:T(8,128)(2,1)S(1)}, u32[]{:S(2)}, u32[]{:S(2)}) %collective-permute-start.17) | collective-permute-done | bytes 393248 | tf_op jit(solution)/shard_map/ppermute | solution.py:212
  205.5 1.0 shard_map.108
  (78 shorter events, 12.2 us)
Async XLA Ops:
  1.2 23.4 %collective-permute-start.19 = (bf16[64,3072]{1,0:T(8,128)(2,1)S(1)}, bf16[64,3072]{1,0:T(8,128)(2,1)S(1)}, u32[]{:S(2)}, u32[]{:S(2)}) collective-permute-start(bf16[64,3072]{1,0:T(8,128)(2,1)S(1)} %get-tuple-element.80.own.x), channel_id=1, source_target_pairs={{0,8},{8,0},{4,12},{12,4},{1,9},{9,1},{5,13},{13,5},{2,10},{10,2},... | collective-permute-start | bytes 1179656 | tf_op jit(solution)/shard_map/ppermute | solution.py:212
  5.3 20.8 %collective-permute-start.18 = (bf16[64,3072]{1,0:T(8,128)(2,1)S(1)}, bf16[64,3072]{1,0:T(8,128)(2,1)S(1)}, u32[]{:S(2)}, u32[]{:S(2)}) collective-permute-start(bf16[64,3072]{1,0:T(8,128)(2,1)S(1)} %get-tuple-element.80.own.x), channel_id=1, source_target_pairs={{0,4},{4,0},{8,12},{12,8},{1,5},{5,1},{9,13},{13,9},{2,6},{6,2},{1... | collective-permute-start | bytes 1179656 | tf_op jit(solution)/shard_map/ppermute | solution.py:212
  6.8 43.5 %collective-permute-start.20 = (bf16[64,3072]{1,0:T(8,128)(2,1)S(1)}, bf16[64,3072]{1,0:T(8,128)(2,1)S(1)}, u32[]{:S(2)}, u32[]{:S(2)}) collective-permute-start(bf16[64,3072]{1,0:T(8,128)(2,1)S(1)} %get-tuple-element.80.own.x), channel_id=1, source_target_pairs={{4,8},{8,4},{5,9},{9,5},{6,10},{10,6},{7,11},{11,7},{20,24},{24,20... | collective-permute-start | bytes 1179656 | tf_op jit(solution)/shard_map/ppermute | solution.py:212
  7.5 41.5 %collective-permute-start.1 = (bf16[64,3072]{1,0:T(8,128)(2,1)S(1)}, bf16[64,3072]{1,0:T(8,128)(2,1)S(1)}, u32[]{:S(2)}, u32[]{:S(2)}) collective-permute-start(bf16[64,3072]{1,0:T(8,128)(2,1)S(1)} %get-tuple-element.81.own.x), channel_id=1, source_target_pairs={{0,8},{8,0},{4,12},{12,4},{1,9},{9,1},{5,13},{13,5},{2,10},{10,2},... | collective-permute-start | bytes 1179656 | tf_op jit(solution)/shard_map/ppermute | solution.py:212
  10.7 46.7 %collective-permute-start = (bf16[64,3072]{1,0:T(8,128)(2,1)S(1)}, bf16[64,3072]{1,0:T(8,128)(2,1)S(1)}, u32[]{:S(2)}, u32[]{:S(2)}) collective-permute-start(bf16[64,3072]{1,0:T(8,128)(2,1)S(1)} %get-tuple-element.81.own.x), channel_id=1, source_target_pairs={{0,4},{4,0},{8,12},{12,8},{1,5},{5,1},{9,13},{13,9},{2,6},{6,2},{1... | collective-permute-start | bytes 1179656 | tf_op jit(solution)/shard_map/ppermute | solution.py:212
  24.6 25.8 %collective-permute-start.21 = (bf16[64,3072]{1,0:T(8,128)(2,1)S(1)}, bf16[64,3072]{1,0:T(8,128)(2,1)S(1)}, u32[]{:S(2)}, u32[]{:S(2)}) collective-permute-start(bf16[64,3072]{1,0:T(8,128)(2,1)S(1)} %collective-permute-done.19.far), channel_id=1, source_target_pairs={{4,0},{8,12},{5,1},{9,13},{6,2},{10,14},{7,3},{11,15},{20,16},{24,... | collective-permute-start | bytes 1179656 | tf_op jit(solution)/shard_map/ppermute | solution.py:212
  26.0 31.7 %collective-permute-start.2 = (bf16[64,3072]{1,0:T(8,128)(2,1)S(1)}, bf16[64,3072]{1,0:T(8,128)(2,1)S(1)}, u32[]{:S(2)}, u32[]{:S(2)}) collective-permute-start(bf16[64,3072]{1,0:T(8,128)(2,1)S(1)} %get-tuple-element.81.own.x), channel_id=1, source_target_pairs={{4,8},{8,4},{5,9},{9,5},{6,10},{10,6},{7,11},{11,7},{20,24},{24,20... | collective-permute-start | bytes 1179656 | tf_op jit(solution)/shard_map/ppermute | solution.py:212
  49.0 11.4 %collective-permute-start.3 = (bf16[64,3072]{1,0:T(8,128)(2,1)S(1)}, bf16[64,3072]{1,0:T(8,128)(2,1)S(1)}, u32[]{:S(2)}, u32[]{:S(2)}) collective-permute-start(bf16[64,3072]{1,0:T(8,128)(2,1)S(1)} %collective-permute-done.1.far), channel_id=1, source_target_pairs={{4,0},{8,12},{5,1},{9,13},{6,2},{10,14},{7,3},{11,15},{20,16},{24,... | collective-permute-start | bytes 1179656 | tf_op jit(solution)/shard_map/ppermute | solution.py:212
  50.3 0.7 copy-start
  51.1 1.0 copy-start.1
  55.5 12.1 %collective-permute-start.23 = (bf16[64,3072]{1,0:T(8,128)(2,1)S(1)}, bf16[64,3072]{1,0:T(8,128)(2,1)S(1)}, u32[]{:S(2)}, u32[]{:S(2)}) collective-permute-start(bf16[64,3072]{1,0:T(8,128)(2,1)S(1)} %get-tuple-element.62), channel_id=1, source_target_pairs={{0,2},{2,0},{1,3},{3,1},{4,6},{6,4},{5,7},{7,5},{8,10},{10,8},{9,1... | collective-permute-start | bytes 1179656 | tf_op jit(solution)/shard_map/ppermute | solution.py:212
  57.3 18.1 %collective-permute-start.24 = (bf16[64,3072]{1,0:T(8,128)(2,1)}, bf16[64,3072]{1,0:T(8,128)(2,1)}, u32[]{:S(2)}, u32[]{:S(2)}) collective-permute-start(bf16[64,3072]{1,0:T(8,128)(2,1)} %get-tuple-element.63), channel_id=1, source_target_pairs={{0,3},{3,0},{1,2},{2,1},{4,7},{7,4},{5,6},{6,5},{8,11},{11,8},{9,1... | collective-permute-start | bytes 1179656 | tf_op jit(solution)/shard_map/ppermute | solution.py:212
  57.4 22.4 %collective-permute-start.22 = (bf16[64,3072]{1,0:T(8,128)(2,1)}, bf16[64,3072]{1,0:T(8,128)(2,1)S(1)}, u32[]{:S(2)}, u32[]{:S(2)}) collective-permute-start(bf16[64,3072]{1,0:T(8,128)(2,1)} %get-tuple-element.60), channel_id=1, source_target_pairs={{0,1},{1,0},{2,3},{3,2},{4,5},{5,4},{6,7},{7,6},{8,9},{9,8},{10,11... | collective-permute-start | bytes 1179656 | tf_op jit(solution)/shard_map/ppermute | solution.py:212
  63.9 20.5 %collective-permute-start.5 = (bf16[64,3072]{1,0:T(8,128)(2,1)}, bf16[64,3072]{1,0:T(8,128)(2,1)S(1)}, u32[]{:S(2)}, u32[]{:S(2)}) collective-permute-start(bf16[64,3072]{1,0:T(8,128)(2,1)} %get-tuple-element.44), channel_id=1, source_target_pairs={{0,2},{2,0},{1,3},{3,1},{4,6},{6,4},{5,7},{7,5},{8,10},{10,8},{9,1... | collective-permute-start | bytes 1179656 | tf_op jit(solution)/shard_map/ppermute | solution.py:212
  65.2 23.9 %collective-permute-start.6 = (bf16[64,3072]{1,0:T(8,128)(2,1)}, bf16[64,3072]{1,0:T(8,128)(2,1)}, u32[]{:S(2)}, u32[]{:S(2)}) collective-permute-start(bf16[64,3072]{1,0:T(8,128)(2,1)} %get-tuple-element.45), channel_id=1, source_target_pairs={{0,3},{3,0},{1,2},{2,1},{4,7},{7,4},{5,6},{6,5},{8,11},{11,8},{9,1... | collective-permute-start | bytes 1179656 | tf_op jit(solution)/shard_map/ppermute | solution.py:212
  67.5 26.3 %collective-permute-start.4 = (bf16[64,3072]{1,0:T(8,128)(2,1)}, bf16[64,3072]{1,0:T(8,128)(2,1)S(1)}, u32[]{:S(2)}, u32[]{:S(2)}) collective-permute-start(bf16[64,3072]{1,0:T(8,128)(2,1)} %get-tuple-element.42), channel_id=1, source_target_pairs={{0,1},{1,0},{2,3},{3,2},{4,5},{5,4},{6,7},{7,6},{8,9},{9,8},{10,11... | collective-permute-start | bytes 1179656 | tf_op jit(solution)/shard_map/ppermute | solution.py:212
  79.7 18.7 %collective-permute-start.26 = (bf16[64,512]{1,0:T(8,128)(2,1)S(1)}, bf16[64,512]{1,0:T(8,128)(2,1)S(1)}, u32[]{:S(2)}, u32[]{:S(2)}) collective-permute-start(bf16[64,512]{1,0:T(8,128)(2,1)S(1)} %get-tuple-element.66), channel_id=1, source_target_pairs={{0,1},{1,0},{2,3},{3,2},{4,5},{5,4},{6,7},{7,6},{8,9},{9,8},{10,11... | collective-permute-start | bytes 196616 | tf_op jit(solution)/shard_map/ppermute | solution.py:212
  83.7 14.7 %collective-permute-start.25 = (bf16[64,512]{1,0:T(8,128)(2,1)S(1)}, bf16[64,512]{1,0:T(8,128)(2,1)S(1)}, u32[]{:S(2)}, u32[]{:S(2)}) collective-permute-start(bf16[64,512]{1,0:T(8,128)(2,1)S(1)} %get-tuple-element.65), channel_id=1, source_target_pairs={{0,1},{1,0},{2,3},{3,2},{4,5},{5,4},{6,7},{7,6},{8,9},{9,8},{10,11... | collective-permute-start | bytes 196616 | tf_op jit(solution)/shard_map/ppermute | solution.py:212
  93.4 6.4 %collective-permute-start.8 = (bf16[64,512]{1,0:T(8,128)(2,1)S(1)}, bf16[64,512]{1,0:T(8,128)(2,1)S(1)}, u32[]{:S(2)}, u32[]{:S(2)}) collective-permute-start(bf16[64,512]{1,0:T(8,128)(2,1)S(1)} %get-tuple-element.48), channel_id=1, source_target_pairs={{0,1},{1,0},{2,3},{3,2},{4,5},{5,4},{6,7},{7,6},{8,9},{9,8},{10,11... | collective-permute-start | bytes 196616 | tf_op jit(solution)/shard_map/ppermute | solution.py:212
  97.7 2.0 collective-permute-start.7
  98.4 6.4 %collective-permute-start.27 = (bf16[128,512]{1,0:T(8,128)(2,1)S(1)}, bf16[128,512]{1,0:T(8,128)(2,1)S(1)}, u32[]{:S(2)}, u32[]{:S(2)}) collective-permute-start(bf16[128,512]{1,0:T(8,128)(2,1)S(1)} %get-tuple-element.68), channel_id=1, source_target_pairs={{0,2},{2,0},{1,3},{3,1},{4,6},{6,4},{5,7},{7,5},{8,10},{10,8},{9,1... | collective-permute-start | bytes 393224 | tf_op jit(solution)/shard_map/ppermute | solution.py:212
  99.8 7.4 %collective-permute-start.9 = (bf16[128,512]{1,0:T(8,128)(2,1)S(1)}, bf16[128,512]{1,0:T(8,128)(2,1)S(1)}, u32[]{:S(2)}, u32[]{:S(2)}) collective-permute-start(bf16[128,512]{1,0:T(8,128)(2,1)S(1)} %get-tuple-element.50), channel_id=1, source_target_pairs={{0,2},{2,0},{1,3},{3,1},{4,6},{6,4},{5,7},{7,5},{8,10},{10,8},{9,1... | collective-permute-start | bytes 393224 | tf_op jit(solution)/shard_map/ppermute | solution.py:212
  105.4 2.5 %collective-permute-start.28 = (bf16[128,512]{1,0:T(8,128)(2,1)S(1)}, bf16[128,512]{1,0:T(8,128)(2,1)S(1)}, u32[]{:S(2)}, u32[]{:S(2)}) collective-permute-start(bf16[128,512]{1,0:T(8,128)(2,1)S(1)} %shard_map.103), channel_id=1, source_target_pairs={{0,1},{1,0},{2,3},{3,2},{4,5},{5,4},{6,7},{7,6},{8,9},{9,8},{10,11... | collective-permute-start | bytes 393224 | tf_op jit(solution)/shard_map/ppermute | solution.py:212
  107.8 9.6 %collective-permute-start.10 = (bf16[128,512]{1,0:T(8,128)(2,1)S(1)}, bf16[128,512]{1,0:T(8,128)(2,1)S(1)}, u32[]{:S(2)}, u32[]{:S(2)}) collective-permute-start(bf16[128,512]{1,0:T(8,128)(2,1)S(1)} %shard_map.95), channel_id=1, source_target_pairs={{0,1},{1,0},{2,3},{3,2},{4,5},{5,4},{6,7},{7,6},{8,9},{9,8},{10,11... | collective-permute-start | bytes 393224 | tf_op jit(solution)/shard_map/ppermute | solution.py:212
  111.8 14.7 %collective-permute-start.30 = (bf16[64,3072]{1,0:T(8,128)(2,1)S(1)}, bf16[64,3072]{1,0:T(8,128)(2,1)S(1)}, u32[]{:S(2)}, u32[]{:S(2)}) collective-permute-start(bf16[64,3072]{1,0:T(8,128)(2,1)S(1)} %get-tuple-element.71), channel_id=1, source_target_pairs={{0,2},{2,0},{1,3},{3,1},{4,6},{6,4},{5,7},{7,5},{8,10},{10,8},{9,1... | collective-permute-start | bytes 1179656 | tf_op jit(solution)/shard_map/ppermute | solution.py:212
  113.1 17.9 %collective-permute-start.31 = (bf16[64,3072]{1,0:T(8,128)(2,1)S(1)}, bf16[64,3072]{1,0:T(8,128)(2,1)S(1)}, u32[]{:S(2)}, u32[]{:S(2)}) collective-permute-start(bf16[64,3072]{1,0:T(8,128)(2,1)S(1)} %get-tuple-element.72), channel_id=1, source_target_pairs={{0,3},{3,0},{1,2},{2,1},{4,7},{7,4},{5,6},{6,5},{8,11},{11,8},{9,1... | collective-permute-start | bytes 1179656 | tf_op jit(solution)/shard_map/ppermute | solution.py:212
  117.1 13.9 %collective-permute-start.29 = (bf16[64,3072]{1,0:T(8,128)(2,1)S(1)}, bf16[64,3072]{1,0:T(8,128)(2,1)S(1)}, u32[]{:S(2)}, u32[]{:S(2)}) collective-permute-start(bf16[64,3072]{1,0:T(8,128)(2,1)S(1)} %get-tuple-element.70), channel_id=1, source_target_pairs={{0,1},{1,0},{2,3},{3,2},{4,5},{5,4},{6,7},{7,6},{8,9},{9,8},{10,11... | collective-permute-start | bytes 1179656 | tf_op jit(solution)/shard_map/ppermute | solution.py:212
  117.5 64.3 %copy-start.2 = (bf16[3072]{0:T(1024)(128)(2,1)S(1)}, bf16[3072]{0:T(1024)(128)(2,1)}, u32[]{:S(2)}) copy-start(bf16[3072]{0:T(1024)(128)(2,1)} %param.15) | copy-start | bytes 18436
  121.3 19.3 %collective-permute-start.12 = (bf16[64,3072]{1,0:T(8,128)(2,1)S(1)}, bf16[64,3072]{1,0:T(8,128)(2,1)S(1)}, u32[]{:S(2)}, u32[]{:S(2)}) collective-permute-start(bf16[64,3072]{1,0:T(8,128)(2,1)S(1)} %get-tuple-element.53), channel_id=1, source_target_pairs={{0,2},{2,0},{1,3},{3,1},{4,6},{6,4},{5,7},{7,5},{8,10},{10,8},{9,1... | collective-permute-start | bytes 1179656 | tf_op jit(solution)/shard_map/ppermute | solution.py:212
  122.6 24.6 %collective-permute-start.13 = (bf16[64,3072]{1,0:T(8,128)(2,1)S(1)}, bf16[64,3072]{1,0:T(8,128)(2,1)S(1)}, u32[]{:S(2)}, u32[]{:S(2)}) collective-permute-start(bf16[64,3072]{1,0:T(8,128)(2,1)S(1)} %get-tuple-element.54), channel_id=1, source_target_pairs={{0,3},{3,0},{1,2},{2,1},{4,7},{7,4},{5,6},{6,5},{8,11},{11,8},{9,1... | collective-permute-start | bytes 1179656 | tf_op jit(solution)/shard_map/ppermute | solution.py:212
  126.5 20.8 %collective-permute-start.11 = (bf16[64,3072]{1,0:T(8,128)(2,1)S(1)}, bf16[64,3072]{1,0:T(8,128)(2,1)S(1)}, u32[]{:S(2)}, u32[]{:S(2)}) collective-permute-start(bf16[64,3072]{1,0:T(8,128)(2,1)S(1)} %get-tuple-element.52), channel_id=1, source_target_pairs={{0,1},{1,0},{2,3},{3,2},{4,5},{5,4},{6,7},{7,6},{8,9},{9,8},{10,11... | collective-permute-start | bytes 1179656 | tf_op jit(solution)/shard_map/ppermute | solution.py:212
  131.8 27.1 %collective-permute-start.34 = (bf16[64,3072]{1,0:T(8,128)(2,1)S(1)}, bf16[64,3072]{1,0:T(8,128)(2,1)S(1)}, u32[]{:S(2)}, u32[]{:S(2)}) collective-permute-start(bf16[64,3072]{1,0:T(8,128)(2,1)S(1)} %get-tuple-element.75), channel_id=1, source_target_pairs={{0,4},{12,8},{1,5},{13,9},{2,6},{14,10},{3,7},{15,11},{16,20},{28,... | collective-permute-start | bytes 1179656 | tf_op jit(solution)/shard_map/ppermute | solution.py:212
  136.8 44.9 %collective-permute-start.33 = (bf16[64,3072]{1,0:T(8,128)(2,1)S(1)}, bf16[64,3072]{1,0:T(8,128)(2,1)S(1)}, u32[]{:S(2)}, u32[]{:S(2)}) collective-permute-start(bf16[64,3072]{1,0:T(8,128)(2,1)S(1)} %get-tuple-element.75), channel_id=1, source_target_pairs={{4,8},{8,4},{5,9},{9,5},{6,10},{10,6},{7,11},{11,7},{20,24},{24,20... | collective-permute-start | bytes 1179656 | tf_op jit(solution)/shard_map/ppermute | solution.py:212
  148.0 15.1 %collective-permute-start.16 = (bf16[64,3072]{1,0:T(8,128)(2,1)S(1)}, bf16[64,3072]{1,0:T(8,128)(2,1)S(1)}, u32[]{:S(2)}, u32[]{:S(2)}) collective-permute-start(bf16[64,3072]{1,0:T(8,128)(2,1)S(1)} %get-tuple-element.57), channel_id=1, source_target_pairs={{0,4},{12,8},{1,5},{13,9},{2,6},{14,10},{3,7},{15,11},{16,20},{28,... | collective-permute-start | bytes 1179656 | tf_op jit(solution)/shard_map/ppermute | solution.py:212
  153.7 35.8 %collective-permute-start.15 = (bf16[64,3072]{1,0:T(8,128)(2,1)S(1)}, bf16[64,3072]{1,0:T(8,128)(2,1)S(1)}, u32[]{:S(2)}, u32[]{:S(2)}) collective-permute-start(bf16[64,3072]{1,0:T(8,128)(2,1)S(1)} %get-tuple-element.57), channel_id=1, source_target_pairs={{4,8},{8,4},{5,9},{9,5},{6,10},{10,6},{7,11},{11,7},{20,24},{24,20... | collective-permute-start | bytes 1179656 | tf_op jit(solution)/shard_map/ppermute | solution.py:212
  154.4 27.0 %collective-permute-start.32 = (bf16[64,3072]{1,0:T(8,128)(2,1)S(1)}, bf16[64,3072]{1,0:T(8,128)(2,1)S(1)}, u32[]{:S(2)}, u32[]{:S(2)}) collective-permute-start(bf16[64,3072]{1,0:T(8,128)(2,1)S(1)} %get-tuple-element.74), channel_id=1, source_target_pairs={{0,4},{4,0},{8,12},{12,8},{1,5},{5,1},{9,13},{13,9},{2,6},{6,2},{1... | collective-permute-start | bytes 1179656 | tf_op jit(solution)/shard_map/ppermute | solution.py:212
  158.8 30.6 %collective-permute-start.14 = (bf16[64,3072]{1,0:T(8,128)(2,1)S(1)}, bf16[64,3072]{1,0:T(8,128)(2,1)S(1)}, u32[]{:S(2)}, u32[]{:S(2)}) collective-permute-start(bf16[64,3072]{1,0:T(8,128)(2,1)S(1)} %get-tuple-element.56), channel_id=1, source_target_pairs={{0,4},{4,0},{8,12},{12,8},{1,5},{5,1},{9,13},{13,9},{2,6},{6,2},{1... | collective-permute-start | bytes 1179656 | tf_op jit(solution)/shard_map/ppermute | solution.py:212
  163.1 25.3 %collective-permute-start.35 = (bf16[64,3072]{1,0:T(8,128)(2,1)S(1)}, bf16[64,3072]{1,0:T(8,128)(2,1)S(1)}, u32[]{:S(2)}, u32[]{:S(2)}) collective-permute-start(bf16[64,3072]{1,0:T(8,128)(2,1)S(1)} %add_convert_fusion), channel_id=1, source_target_pairs={{0,8},{8,0},{4,12},{12,4},{1,9},{9,1},{5,13},{13,5},{2,10},{10,2},... | collective-permute-start | bytes 1179656 | tf_op jit(solution)/shard_map/ppermute | solution.py:212
  181.4 24.1 %collective-permute-start.17 = (bf16[64,3072]{1,0:T(8,128)(2,1)S(1)}, bf16[64,3072]{1,0:T(8,128)(2,1)S(1)}, u32[]{:S(2)}, u32[]{:S(2)}) collective-permute-start(bf16[64,3072]{1,0:T(8,128)(2,1)S(1)} %add_convert_fusion.1), channel_id=1, source_target_pairs={{0,8},{8,0},{4,12},{12,4},{1,9},{9,1},{5,13},{13,5},{2,10},{10,2},... | collective-permute-start | bytes 1179656 | tf_op jit(solution)/shard_map/ppermute | solution.py:212

commit v2 on v1

v2 whole, which is shorter than its diff:
```python
import functools

import jax
import jax.numpy as jnp
from jax import lax
from jax.experimental import pallas as pl
from jax.experimental.pallas import tpu as pltpu
from jax.sharding import PartitionSpec as P

BLOCK = 128
CAP = 4
PIECES = (3, 3, 2)
DIRECT_IN = ()
MID_LATE = ()
NEAR_LATE = ()
DIRECT_OUT = ()
ORDER = (
    "Z0 P W0 Z1",
    "Q N0 W1 Z2",
    "U0 N1 W2 D0",
    "U1 N2 R0 D1",
    "U2 J0 R1 D2",
    "E0 J1 R2 E1",
    "J2 E2",
)
bf16 = jnp.bfloat16
f32 = jnp.float32

VMEM = pl.BlockSpec(memory_space=pltpu.VMEM)
SMEM = pl.BlockSpec(memory_space=pltpu.SMEM)
ANY = pl.BlockSpec(memory_space=pl.ANY)


def call(body, outs, in_specs, out_specs=None, scratch=(), flops=0, moved=0, aliases=None, grid=(), limit=7):
    return pl.pallas_call(
        body,
        grid=grid,
        out_shape=outs,
        in_specs=in_specs,
        out_specs=out_specs if out_specs is not None else jax.tree.map(lambda _: VMEM, outs),
        scratch_shapes=list(scratch),
        input_output_aliases=aliases or {},
        compiler_params=pltpu.CompilerParams(vmem_limit_bytes=limit * 1024 * 1024),
        cost_estimate=pl.CostEstimate(flops=0, bytes_accessed=0, transcendentals=0),
    )


def slots(active_ids, active_counts, local_blocks, tensor_index):
    slot_total = active_ids.shape[1]
    local_ids = active_ids - tensor_index * local_blocks
    present = (
        (jnp.arange(slot_total)[None, :] < active_counts[:, None])
        & (local_ids >= 0)
        & (local_ids < local_blocks)
    )
    present_int = present.astype(jnp.int32)
    position = jnp.cumsum(present_int, axis=1) - 1
    matches = present_int[:, :, None] * (
        position[:, :, None] == jnp.arange(CAP)[None, None, :]
    ).astype(jnp.int32)
    slot_block = jnp.sum(matches * local_ids[:, :, None], axis=1)
    live_total = jnp.sum(present_int, axis=1)
    return slot_block, live_total


def norm_kernel(n, where_ref, gain, shift, own, near, far, *rest):
    last, outs, scr = rest[:n], rest[n : n + 4], rest[n + 4]
    rows, width = own.shape
    step = 16
    lanes = 512 if width % 512 == 0 else 128
    cuts = [pl.ds(c, lanes) for c in range(0, width, lanes)]
    t, s = where_ref[0], where_ref[1]
    full = 4 * width

    def chunk(i, _):
        at = pl.ds(pl.multiple_of(i * step, step), step)

        def part(k, cut):
            if k < 3:
                return (own, near, far)[k][at, cut].astype(f32)
            return sum(ref[at, cut].astype(f32) for ref in last)

        def mean(term):
            sums = []
            for k in range(4):
                acc = term(part(k, cuts[0]))
                for cut in cuts[1:]:
                    acc = acc + term(part(k, cut))
                sums.append(acc)
            return jnp.sum(sum(sums), axis=1, keepdims=True) / full

        center = mean(lambda v: v)
        factor = lax.rsqrt(mean(lambda v: jnp.square(v - center)) + 1e-05)
        for k in range(4):
            f = jnp.bitwise_xor(t, k)
            j = jnp.bitwise_xor(s, k)
            for cut in cuts:
                scaled = (part(k, cut) - center) * factor
                scr[j, at, cut] = (scaled * gain[f, :, cut] + shift[f, :, cut]).astype(bf16)
        return 0

    lax.fori_loop(0, rows // step, chunk, 0)
    for j in range(4):
        outs[j][...] = scr[j]


def normalize(where, parts, gain, shift):
    shape = parts[0].shape
    out = jax.ShapeDtypeStruct(shape, bf16)
    return call(
        functools.partial(norm_kernel, len(parts) - 3),
        [out] * 4,
        [SMEM] + [VMEM] * (len(parts) + 2),
        scratch=[pltpu.VMEM((4,) + shape, bf16)],
    )(where, gain, shift, *parts)


def pack_kernel(groups, rows_packed, sid, live, w, *refs):
    outs, sems = refs[:-1], refs[-1]
    copies = []
    for out, group in zip(outs, groups):
        for q, j in enumerate(group):
            for k in range(CAP):
                at = pl.ds(pl.multiple_of(sid[j, k] * BLOCK, BLOCK), BLOCK)
                to = pl.ds(k * BLOCK, BLOCK)
                if rows_packed:
                    source, target = w.at[at, :], out.at[q, to, :]
                else:
                    source, target = w.at[:, at], out.at[q, :, to]
                on = k < live[j]
                copy = pltpu.make_async_copy(source, target, sems.at[j, k])
                pl.when(on)(copy.start)

                @pl.when(jnp.logical_not(on))
                def _(target=target):
                    target[...] = jnp.zeros(target.shape, bf16)

                copies.append((on, copy))
    for on, copy in copies:
        pl.when(on)(copy.wait)


def pack(groups, sid, live, w, rows_packed, limit):
    size = CAP * BLOCK
    shape = (size, w.shape[1]) if rows_packed else (w.shape[0], size)
    outs = [jax.ShapeDtypeStruct((len(group),) + shape, bf16) for group in groups]
    return call(
        functools.partial(pack_kernel, groups, rows_packed),
        outs,
        [SMEM, SMEM, ANY],
        scratch=[pltpu.SemaphoreType.DMA((live.shape[0], CAP))],
        limit=limit,
    )(sid, live, w)


def product_kernel(n, *refs):
    xs, w, outs = refs[:n], refs[n], refs[n + 1 :]
    for q in range(n):
        outs[q][...] = jnp.dot(xs[q][...], w[q], preferred_element_type=f32).astype(outs[q].dtype)


def product(kinds, xs, w):
    n = len(xs)
    rows = xs[0].shape[0]
    width = w.shape[2]
    return call(
        functools.partial(product_kernel, n),
        [jax.ShapeDtypeStruct((rows, width), kind) for kind in kinds],
        [VMEM] * (n + 1),
        flops=n * rows * w.shape[1] * width * 2,
        moved=n * w.shape[1] * width * 2,
        limit=8,
    )(*xs, w)


def pair_kernel(p0, p2, r1, r3, s_ref, send):
    rows = p0.shape[0]
    for i, (p, r) in enumerate(((p0, r1), (p2, r3))):
        total = p[...] + r[...].astype(f32)
        at = pl.ds(i * rows, rows)
        s_ref[at, :] = total
        send[at, :] = total.astype(bf16)


def hidden_kernel(live, s_ref, got, bias, out):
    rows = s_ref.shape[0] // 2
    lane = lax.broadcasted_iota(jnp.int32, (rows, CAP * BLOCK), 1)
    for i in range(2):
        at, other = pl.ds(i * rows, rows), pl.ds((1 - i) * rows, rows)
        value = s_ref[at, :] + got[other, :].astype(f32) + bias[i]
        on = lane < live[2 * i] * BLOCK
        out[at, :] = jnp.where(on, jnp.maximum(value, 0.0), 0.0).astype(bf16)


def route_kernel(where_ref, y0, y1, y2, y3, z0, z1, z2, z3, scr):
    s = where_ref[1]
    for j, y in enumerate((y0, y1, y2, y3)):
        scr[jnp.bitwise_xor(s, j)] = y[...]
    for k, z in enumerate((z0, z1, z2, z3)):
        z[...] = scr[k]


def final_kernel(start, bias, x, z0, z1, z2, z3, *refs):
    out, scr, sem = refs[-3:]
    total = x[...].astype(f32) + bias[...]
    for z in (z0, z1, z2, z3):
        total = total + z[...].astype(f32)
    scr[...] = total.astype(bf16)
    copy = pltpu.make_async_copy(scr, out.at[pl.ds(start, scr.shape[0]), :], sem)
    copy.start()
    copy.wait()


def swap(x, axis, pairs):
    return lax.ppermute(x, axis, pairs)


NEAR = [(0, 1), (1, 0), (2, 3), (3, 2)]
FAR = [(0, 2), (2, 0), (1, 3), (3, 1)]
CROSS = [(0, 3), (3, 0), (1, 2), (2, 1)]
MIDDLE = [(1, 2), (2, 1)]
OUTWARD = [(1, 0), (2, 3)]
INWARD = [(0, 1), (3, 2)]
PAIRS = ((0, 1), (2, 3))
BATCH = {1: NEAR, 2: FAR, 3: CROSS}


def after(value, token):
    if token is None:
        return value
    return lax.optimization_barrier((value, token))[0]


def small_mesh(
    stream, ln_gain, ln_bias, fc1_weight, fc1_bias, fc2_weight, fc2_bias, active_ids, active_counts
):
    t = lax.axis_index("tensor")
    b = lax.axis_index("batch")
    rows, width = stream.shape
    local_blocks = fc1_weight.shape[1] // BLOCK
    sizes = [rows * n // sum(PIECES) for n in PIECES]
    starts = [sum(sizes[:p]) for p in range(len(sizes))]
    xs = [stream[: sizes[0]]]
    later = after(stream, xs[0])
    xs += [later[i : i + m] for i, m in zip(starts[1:], sizes[1:])]

    slot_block, live_total = slots(active_ids, active_counts, local_blocks, t)
    order = jnp.bitwise_xor(b, jnp.arange(4))
    sid = jnp.take(slot_block, order, axis=0)
    live = jnp.take(live_total, order, axis=0)
    bias_table = fc1_bias.reshape(local_blocks, BLOCK).astype(f32)
    up_bias = jnp.take(bias_table, sid[::2], axis=0).reshape(2, 1, CAP * BLOCK)
    where = jnp.stack([t, jnp.bitwise_xor(t, b)]).astype(jnp.int32)
    gain = ln_gain.astype(f32).reshape(4, 1, width)
    shift = ln_bias.astype(f32).reshape(4, 1, width)
    down_bias = fc2_bias.astype(f32).reshape(1, width)
    up_blocks = pack(PAIRS, sid, live, fc1_weight, False, 27)
    setup = [where, live, up_bias, gain, shift, down_bias, up_blocks]

    held = {}
    token = None

    def send(p):
        x = xs[p] if token is None else after(xs[p], token)
        held[p] = {
            "far": swap(x, "tensor", FAR),
            "near": swap(x, "tensor", NEAR),
            "last": [],
        }
        if p in DIRECT_IN:
            held[p]["last"].append(swap(x, "tensor", CROSS))
        elif p not in MID_LATE:
            held[p]["last"].append(swap(x, "tensor", MIDDLE))

    def forward(p):
        h = held[p]
        if p in DIRECT_IN:
            return None
        far = h["far"] if token is None else after(h["far"], token)
        if p in MID_LATE:
            x = after(xs[p], (far, h["near"]))
            h["last"].append(swap(x, "tensor", MIDDLE))
        h["last"].append(swap(far, "tensor", OUTWARD))
        return far

    def norm(p):
        h = held[p]
        parts = after([xs[p], h["near"], h["far"]] + h["last"], token)
        where, gain, shift = setup[0], setup[3], setup[4]
        n = normalize(where, parts, gain, shift)
        h["n"] = [n[0]] + [swap(n[j], "batch", BATCH[j]) for j in (1, 2, 3)]
        return n[0]

    def first(p):
        h = held[p]
        n = h["n"]
        p0, p1 = product((f32, bf16), after(n[:2], token), setup[6][0])
        r1 = swap(p1, "batch", NEAR)
        p2, p3 = product((f32, bf16), after(n[2:], p0), setup[6][1])
        r3 = swap(p3, "batch", NEAR)
        total = (2 * sizes[p], CAP * BLOCK)
        h["s"], send = call(
            pair_kernel,
            [jax.ShapeDtypeStruct(total, f32), jax.ShapeDtypeStruct(total, bf16)],
            [VMEM] * 4,
        )(p0, p2, r1, r3)
        h["got"] = swap(send, "batch", FAR)
        return h["s"]

    def second(p):
        h = held[p]
        m = sizes[p]
        total = (2 * m, CAP * BLOCK)
        got = after(h["got"], token)
        mine = call(
            hidden_kernel, jax.ShapeDtypeStruct(total, bf16), [SMEM] + [VMEM] * 3, VMEM
        )(setup[1], h["s"], got, setup[2])
        other = swap(mine, "batch", NEAR)
        y2, y3 = product((bf16, bf16), [mine[m:], other[m:]], setup[7][1])
        h["y"] = {j: swap(y, "batch", BATCH[j]) for j, y in ((2, y2), (3, y3))}
        y0, y1 = product((bf16, bf16), after([mine[:m], other[:m]], y2), setup[7][0])
        h["y"][1] = swap(y1, "batch", NEAR)
        h["y"][0] = y0
        return y0

    def route(p):
        h = held[p]
        part = jax.ShapeDtypeStruct((sizes[p], width), bf16)
        ys = after([h["y"][j] for j in range(4)], token)
        z0, z1, z2, z3 = call(
            route_kernel,
            [part] * 4,
            [SMEM] + [VMEM] * 4,
            scratch=[pltpu.VMEM((4, sizes[p], width), bf16)],
        )(setup[0], *ys)
        h["sum"] = [z0]
        if p in DIRECT_OUT:
            h["sum"].append(swap(z2, "tensor", FAR))
            h["sum"].append(swap(z3, "tensor", CROSS))
            h["sum"].append(swap(z1, "tensor", NEAR))
        else:
            h["in"] = swap(z3, "tensor", INWARD)
            h["sum"].append(swap(z3, "tensor", MIDDLE))
            if p not in NEAR_LATE:
                h["sum"].append(swap(z1, "tensor", NEAR))
            h["far"] = z2
            h["near"] = z1
        return z0

    def join(p):
        h = held[p]
        if p in DIRECT_OUT:
            return None
        z2 = h["far"].astype(f32) + after(h["in"], token).astype(f32)
        z2 = z2.astype(bf16)
        if p in NEAR_LATE:
            h["sum"].append(swap(after(h["near"], h["in"]), "tensor", NEAR))
        h["sum"].append(swap(z2, "tensor", FAR))
        return z2

    def finish(p):
        h = held[p]
        m = sizes[p]
        args = [setup[5], xs[p]] + after(h["sum"], token)
        specs = [VMEM] * 6
        aliases = {}
        if "out" in held:
            args.append(held["out"])
            specs.append(ANY)
            aliases = {6: 0}
        held["out"] = call(
            functools.partial(final_kernel, starts[p]),
            jax.ShapeDtypeStruct((rows, width), bf16),
            specs,
            ANY,
            scratch=[pltpu.VMEM((m, width), bf16), pltpu.SemaphoreType.DMA],
            aliases=aliases,
        )(*args)
        return held["out"]

    def check(p):
        held[p]["near"] = after(held[p]["near"], token)
        return held[p]["near"]

    def check_mid(p):
        held[p]["last"][0] = after(held[p]["last"][0], token)
        return held[p]["last"][0]

    steps = {
        "C": check, "M": check_mid, "Z": send, "W": forward, "N": norm, "U": first,
        "D": second, "R": route, "J": join, "E": finish,
    }
    for step in " ".join(ORDER).split():
        if step == "P":
            setup = lax.optimization_barrier(setup)
            token = setup[1]
        elif step == "Q":
            sid = after(sid, token)
            setup.append(pack(PAIRS, sid, live, fc2_weight, True, 16))
            token = setup[7]
        else:
            gate, token = token, None if step[0].islower() else token
            made = steps[step[0].upper()](int(step[1:]))
            token = gate if made is None else made
    return held["out"]


def any_mesh(
    stream, ln_gain, ln_bias, fc1_weight, fc1_bias, fc2_weight, fc2_bias, active_ids, active_counts
):
    batches = lax.axis_size("batch")
    whole_rows = lax.all_gather(stream, "tensor", axis=1, tiled=True)
    values = whole_rows.astype(f32)
    center = jnp.mean(values, axis=-1, keepdims=True)
    spread = jnp.mean(jnp.square(values - center), axis=-1, keepdims=True)
    scaled = (values - center) * lax.rsqrt(spread + 1e-05)
    normed = (scaled * ln_gain.astype(f32) + ln_bias.astype(f32)).astype(bf16)
    columns = lax.all_to_all(normed, "batch", split_axis=1, concat_axis=0, tiled=True)
    rows = stream.shape[0]
    local_blocks = fc1_weight.shape[1] // BLOCK
    sid, live = slots(active_ids, active_counts, local_blocks, lax.axis_index("tensor"))
    bias_table = fc1_bias.reshape(local_blocks, BLOCK).astype(f32)
    bias = jnp.take(bias_table, sid, axis=0).reshape(batches, 1, CAP * BLOCK)
    on = jnp.arange(CAP * BLOCK)[None, None, :] < live[:, None, None] * BLOCK
    parts = []
    for r in range(batches):
        (block,) = pack(((r,),), sid, live, fc1_weight, False, 16)
        parts += product((f32,), [columns[r * rows : (r + 1) * rows]], block)
    share = lax.psum_scatter(jnp.stack(parts), "batch", scatter_dimension=0, tiled=True)
    index = lax.axis_index("batch")
    my_bias = lax.dynamic_slice_in_dim(bias, index, 1, 0)
    my_on = lax.dynamic_slice_in_dim(on, index, 1, 0)
    mine = jnp.where(my_on, jnp.maximum(share + my_bias, 0.0), 0.0).astype(bf16)
    hidden = lax.all_gather(mine, "batch", axis=0, tiled=True)
    outs = []
    for r in range(batches):
        (block,) = pack(((r,),), sid, live, fc2_weight, True, 16)
        outs += product((bf16,), [hidden[r]], block)
    returned = lax.all_to_all(
        jnp.concatenate(outs), "batch", split_axis=0, concat_axis=1, tiled=True
    )
    summed = lax.psum_scatter(returned.astype(f32), "tensor", scatter_dimension=1, tiled=True)
    return (stream.astype(f32) + summed + fc2_bias.astype(f32)).astype(bf16)


def solution(mesh):
    in_specs = (
        P(("groups", "batch"), "tensor"),
        P(),
        P(),
        P("batch", "tensor"),
        P("tensor"),
        P("tensor", "batch"),
        P("tensor"),
        P("groups", None),
        P("groups"),
    )
    out_specs = P(("groups", "batch"), "tensor")
    body = small_mesh if mesh.shape["tensor"] == 4 and mesh.shape["batch"] == 4 else any_mesh
    return jax.shard_map(body, mesh=mesh, in_specs=in_specs, out_specs=out_specs, check_vma=False)
```

time: 207 us -> 161 us (0.78)
  waiting for transfers between devices: 109 us -> 49.8 us
  starting transfers between devices: 45.5 us -> 67.7 us
  Pallas kernels: 43.4 us -> 34.5 us
    ppermute x36 -> x54, waiting for transfers between devices: 109 us -> 49.8 us  [swap(): return lax.ppermute(x, axis, pairs)]
    ppermute x36 -> x54, starting transfers between devices: 45.5 us -> 67.7 us  [swap(): return lax.ppermute(x, axis, pairs)]
    pallas_call x18 -> x29, Pallas kernels: 43.4 us -> 34.5 us  [the longest x12 14.1 us: product(): call(functools.partial(product_kernel, n), [jax.ShapeDtypeStruct((rows, w...]
  transfers between devices with their start and end apart: 36 -> 54, of which waited for: 16 -> 20; matrix products, arithmetic and copies ran while one was open for 3% -> 4% of each run, Pallas kernels for 20% -> 21%
where the time goes in v2:
time: 161 us; the launch traced here: 160 us
  starting transfers between devices  67.7 us (42%)
  waiting for transfers between devices  49.8 us (31%)
  Pallas kernels  34.5 us (21%)
  other arithmetic  4.59 us (3%)
  local copies, waits for them, and re-layouts  2.94 us (2%)
    ppermute x54, starting transfers between devices, swap(): return lax.ppermute(x, axis, pairs)  67.7 us
    ppermute x54, waiting for transfers between devices, swap(): return lax.ppermute(x, axis, pairs)  49.8 us
    pallas_call x12, Pallas kernels, product(): call(functools.partial(product_kernel, n), [jax.ShapeDtypeStruct((rows, w...  14.1 us
    pallas_call x2, Pallas kernels, pack(): call(functools.partial(pack_kernel, groups, rows_packed), outs, [SMEM, SM...  8.62 us
    pallas_call x3, Pallas kernels, normalize(): call(functools.partial(norm_kernel, len(parts) - 3), [out] * 4, [SMEM] +...  5.22 us
  transfers between devices with their start and end apart: 54, of which 20 were waited for; matrix products, arithmetic and copies ran while one was open for 4% of the time, Pallas kernels for 21%

profile of v2, /device:TPU:0, one launch (start us, length us, event | category | flops | bytes accessed | tf_op | source)
XLA Modules:
  0.0 160.4 jit_solution(17117468515339505925)
XLA Ops:
  1.0 4.1 %collective-permute-start = (bf16[48,3072]{1,0:T(8,128)(2,1)S(1)}, bf16[48,3072]{1,0:T(8,128)(2,1)S(1)}, u32[]{:S(2)}, u32[]{:S(2)}) collective-permute-start(bf16[48,3072]{1,0:T(8,128)(2,1)S(1)} %slice.49.own.x), channel_id=1, source_target_pairs={{0,8},{8,0},{4,12},{12,4},{1,9},{9,1},{5,13},{13,5},{2,10},{10,2},... | collective-permute-start | bytes 884744 | tf_op jit(solution)/shard_map/ppermute | solution.py:215
  5.1 1.6 collective-permute-start.2
  13.5 4.4 %shard_map.91 = (bf16[2,3072,512]{2,1,0:T(8,128)(2,1)S(1)}, bf16[2,3072,512]{2,1,0:T(8,128)(2,1)S(1)}) custom-call(s32[4,4]{1,0:T(4,128)S(1)} %broadcast_select_fusion.1.sid, s32[4]{0:T(128)S(1)} %broadcast_select_fusion.2.live, bf16[3072,6144]{1,0:T(8,128)(2,1)} %w.2), custom_call_target="tpu_custom_call" | custom-call | tf_op jit(solution)/shard_map/pallas_call | solution.py:147
  18.1 1.2 collective-permute-done.far
  19.3 1.3 collective-permute-start.4
  20.6 4.0 %collective-permute-start.1 = (bf16[48,3072]{1,0:T(8,128)(2,1)S(1)}, bf16[48,3072]{1,0:T(8,128)(2,1)S(1)}, u32[]{:S(2)}, u32[]{:S(2)}) collective-permute-start(bf16[48,3072]{1,0:T(8,128)(2,1)S(1)} %slice.51.own.x), channel_id=1, source_target_pairs={{0,8},{8,0},{4,12},{12,4},{1,9},{9,1},{5,13},{13,5},{2,10},{10,2},... | collective-permute-start | bytes 884744 | tf_op jit(solution)/shard_map/ppermute | solution.py:215
  24.6 4.2 %shard_map.92 = (bf16[2,512,3072]{2,1,0:T(8,128)(2,1)S(1)}, bf16[2,512,3072]{2,1,0:T(8,128)(2,1)S(1)}) custom-call(s32[4,4]{1,0:T(4,128)S(1)} %broadcast_select_fusion.1.sid, s32[4]{0:T(128)S(1)} %broadcast_select_fusion.2.live, bf16[6144,3072]{1,0:T(8,128)(2,1)} %w.3), custom_call_target="tpu_custom_call" | custom-call | tf_op jit(solution)/shard_map/pallas_call | solution.py:147
  28.9 1.9 %shard_map.93 = (bf16[48,3072]{1,0:T(8,128)(2,1)S(1)}, bf16[48,3072]{1,0:T(8,128)(2,1)S(1)}, bf16[48,3072]{1,0:T(8,128)(2,1)S(1)}, bf16[48,3072]{1,0:T(8,128)(2,1)S(1)}) custom-call(s32[2]{0:T(128)S(1)} %pad_add_fusion.where_ref, f32[4,1,3072]{2,1,0:T(1,128)S(1)} %bitcast.12, f32[4,1,3072]{2,1,0:T(1,128)S(1)} %bitcast.15, bf16[48,3072]{1,0:T(8,128)(2,1)S(1)} %slice.49.own.x, ...), custom_call_target="tpu_custom_call" | custom-call | tf_op jit(solution)/shard_map/pallas_call | solution.py:110
  30.9 1.6 collective-permute-start.12
  32.7 2.9 %collective-permute-start.8 = (bf16[48,3072]{1,0:T(8,128)(2,1)S(1)}, bf16[48,3072]{1,0:T(8,128)(2,1)S(1)}, u32[]{:S(2)}, u32[]{:S(2)}) collective-permute-start(bf16[48,3072]{1,0:T(8,128)(2,1)S(1)} %slice.51.own.x), channel_id=1, source_target_pairs={{0,4},{4,0},{8,12},{12,8},{1,5},{5,1},{9,13},{13,9},{2,6},{6,2},{1... | collective-permute-start | bytes 884744 | tf_op jit(solution)/shard_map/ppermute | solution.py:215
  35.7 1.8 %collective-permute-done.1.far = bf16[48,3072]{1,0:T(8,128)(2,1)S(1)} collective-permute-done((bf16[48,3072]{1,0:T(8,128)(2,1)S(1)}, bf16[48,3072]{1,0:T(8,128)(2,1)S(1)}, u32[]{:S(2)}, u32[]{:S(2)}) %collective-permute-start.1) | collective-permute-done | bytes 294944 | tf_op jit(solution)/shard_map/ppermute | solution.py:215
  38.2 1.3 collective-permute-start.10
  39.5 1.3 collective-permute-done.12.refs_0_
  40.8 3.5 %collective-permute-start.6 = (bf16[32,3072]{1,0:T(8,128)(2,1)S(1)}, bf16[32,3072]{1,0:T(8,128)(2,1)S(1)}, u32[]{:S(2)}, u32[]{:S(2)}) collective-permute-start(bf16[32,3072]{1,0:T(8,128)(2,1)S(1)} %slice.50.own.x), channel_id=1, source_target_pairs={{0,8},{8,0},{4,12},{12,4},{1,9},{9,1},{5,13},{13,5},{2,10},{10,2},... | collective-permute-start | bytes 589832 | tf_op jit(solution)/shard_map/ppermute | solution.py:215
  48.0 1.2 collective-permute-done.15.r3
  49.3 1.6 collective-permute-start.18
  50.9 3.0 %collective-permute-start.5 = (bf16[32,3072]{1,0:T(8,128)(2,1)S(1)}, bf16[32,3072]{1,0:T(8,128)(2,1)S(1)}, u32[]{:S(2)}, u32[]{:S(2)}) collective-permute-start(bf16[32,3072]{1,0:T(8,128)(2,1)S(1)} %slice.50.own.x), channel_id=1, source_target_pairs={{0,4},{4,0},{8,12},{12,8},{1,5},{5,1},{9,13},{13,9},{2,6},{6,2},{1... | collective-permute-start | bytes 589832 | tf_op jit(solution)/shard_map/ppermute | solution.py:215
  53.9 1.9 %shard_map.97 = (bf16[48,3072]{1,0:T(8,128)(2,1)S(1)}, bf16[48,3072]{1,0:T(8,128)(2,1)S(1)}, bf16[48,3072]{1,0:T(8,128)(2,1)S(1)}, bf16[48,3072]{1,0:T(8,128)(2,1)S(1)}) custom-call(s32[2]{0:T(128)S(1)} %pad_add_fusion.where_ref, f32[4,1,3072]{2,1,0:T(1,128)S(1)} %bitcast.13, f32[4,1,3072]{2,1,0:T(1,128)S(1)} %bitcast.16, bf16[48,3072]{1,0:T(8,128)(2,1)S(1)} %slice.51.own.x, ...), custom_call_target="tpu_custom_call" | custom-call | tf_op jit(solution)/shard_map/pallas_call | solution.py:110
  56.9 1.5 collective-permute-start.20
  64.9 1.5 collective-permute-start.27
  67.1 5.1 %collective-permute-done.21.refs_1_ = bf16[48,3072]{1,0:T(8,128)(2,1)S(1)} collective-permute-done((bf16[48,3072]{1,0:T(8,128)(2,1)S(1)}, bf16[48,3072]{1,0:T(8,128)(2,1)S(1)}, u32[]{:S(2)}, u32[]{:S(2)}) %collective-permute-start.21) | collective-permute-done | bytes 294944 | tf_op jit(solution)/shard_map/ppermute | solution.py:215
  75.6 1.3 collective-permute-start.16
  77.0 1.6 collective-permute-start.25
  78.5 6.2 %collective-permute-done.16.rest_1_ = bf16[32,3072]{1,0:T(8,128)(2,1)S(1)} collective-permute-done((bf16[32,3072]{1,0:T(8,128)(2,1)S(1)}, bf16[32,3072]{1,0:T(8,128)(2,1)S(1)}, u32[]{:S(2)}, u32[]{:S(2)}) %collective-permute-start.16) | collective-permute-done | bytes 196640 | tf_op jit(solution)/shard_map/ppermute | solution.py:215
  84.7 1.4 shard_map.104
  86.3 1.5 collective-permute-start.30
  89.9 1.6 %collective-permute-start.38 = (bf16[48,3072]{1,0:T(8,128)(2,1)S(1)}, bf16[48,3072]{1,0:T(8,128)(2,1)S(1)}, u32[]{:S(2)}, u32[]{:S(2)}) collective-permute-start(bf16[48,3072]{1,0:T(8,128)(2,1)S(1)} %get-tuple-element.237), channel_id=1, source_target_pairs={{0,4},{12,8},{1,5},{13,9},{2,6},{14,10},{3,7},{15,11},{16,20},{28,... | collective-permute-start | bytes 884744 | tf_op jit(solution)/shard_map/ppermute | solution.py:215
  92.7 1.2 shard_map.108
  95.1 2.2 %collective-permute-done.31.refs_1_ = bf16[32,3072]{1,0:T(8,128)(2,1)S(1)} collective-permute-done((bf16[32,3072]{1,0:T(8,128)(2,1)S(1)}, bf16[32,3072]{1,0:T(8,128)(2,1)S(1)}, u32[]{:S(2)}, u32[]{:S(2)}) %collective-permute-start.31) | collective-permute-done | bytes 196640 | tf_op jit(solution)/shard_map/ppermute | solution.py:215
  99.7 1.5 collective-permute-start.36
  101.9 1.5 collective-permute-start.34
  103.5 1.2 collective-permute-start.45
  104.7 4.9 %collective-permute-done.36.y2 = bf16[48,3072]{1,0:T(8,128)(2,1)S(1)} collective-permute-done((bf16[48,3072]{1,0:T(8,128)(2,1)S(1)}, bf16[48,3072]{1,0:T(8,128)(2,1)S(1)}, u32[]{:S(2)}, u32[]{:S(2)}) %collective-permute-start.36) | collective-permute-done | bytes 294944 | tf_op jit(solution)/shard_map/ppermute | solution.py:215
  109.6 2.3 %collective-permute-start.46 = (bf16[48,3072]{1,0:T(8,128)(2,1)S(1)}, bf16[48,3072]{1,0:T(8,128)(2,1)S(1)}, u32[]{:S(2)}, u32[]{:S(2)}) collective-permute-start(bf16[48,3072]{1,0:T(8,128)(2,1)S(1)} %add_convert_fusion.1), channel_id=1, source_target_pairs={{0,8},{8,0},{4,12},{12,4},{1,9},{9,1},{5,13},{13,5},{2,10},{10,2},... | collective-permute-start | bytes 884744 | tf_op jit(solution)/shard_map/ppermute | solution.py:215
  111.9 2.9 %collective-permute-done.37.y3 = bf16[48,3072]{1,0:T(8,128)(2,1)S(1)} collective-permute-done((bf16[48,3072]{1,0:T(8,128)(2,1)S(1)}, bf16[48,3072]{1,0:T(8,128)(2,1)S(1)}, u32[]{:S(2)}, u32[]{:S(2)}) %collective-permute-start.37) | collective-permute-done | bytes 294944 | tf_op jit(solution)/shard_map/ppermute | solution.py:215
  117.4 3.1 %collective-permute-start.43 = (bf16[48,3072]{1,0:T(8,128)(2,1)S(1)}, bf16[48,3072]{1,0:T(8,128)(2,1)S(1)}, u32[]{:S(2)}, u32[]{:S(2)}) collective-permute-start(bf16[48,3072]{1,0:T(8,128)(2,1)S(1)} %get-tuple-element.252), channel_id=1, source_target_pairs={{0,4},{12,8},{1,5},{13,9},{2,6},{14,10},{3,7},{15,11},{16,20},{28,... | collective-permute-start | bytes 884744 | tf_op jit(solution)/shard_map/ppermute | solution.py:215
  122.4 1.2 shard_map.115
  123.6 2.4 %collective-permute-start.51 = (bf16[48,3072]{1,0:T(8,128)(2,1)S(1)}, bf16[48,3072]{1,0:T(8,128)(2,1)S(1)}, u32[]{:S(2)}, u32[]{:S(2)}) collective-permute-start(bf16[48,3072]{1,0:T(8,128)(2,1)S(1)} %get-tuple-element.267), channel_id=1, source_target_pairs={{0,4},{4,0},{8,12},{12,8},{1,5},{5,1},{9,13},{13,9},{2,6},{6,2},{1... | collective-permute-start | bytes 884744 | tf_op jit(solution)/shard_map/ppermute | solution.py:215
  126.0 1.4 collective-permute-start.41
  129.3 2.4 %collective-permute-start.52 = (bf16[48,3072]{1,0:T(8,128)(2,1)S(1)}, bf16[48,3072]{1,0:T(8,128)(2,1)S(1)}, u32[]{:S(2)}, u32[]{:S(2)}) collective-permute-start(bf16[48,3072]{1,0:T(8,128)(2,1)S(1)} %add_convert_fusion), channel_id=1, source_target_pairs={{0,8},{8,0},{4,12},{12,4},{1,9},{9,1},{5,13},{13,5},{2,10},{10,2},... | collective-permute-start | bytes 884744 | tf_op jit(solution)/shard_map/ppermute | solution.py:215
  131.6 2.1 %collective-permute-done.41.y2 = bf16[32,3072]{1,0:T(8,128)(2,1)S(1)} collective-permute-done((bf16[32,3072]{1,0:T(8,128)(2,1)S(1)}, bf16[32,3072]{1,0:T(8,128)(2,1)S(1)}, u32[]{:S(2)}, u32[]{:S(2)}) %collective-permute-start.41) | collective-permute-done | bytes 196640 | tf_op jit(solution)/shard_map/ppermute | solution.py:215
  133.7 2.1 %collective-permute-done.42.y3 = bf16[32,3072]{1,0:T(8,128)(2,1)S(1)} collective-permute-done((bf16[32,3072]{1,0:T(8,128)(2,1)S(1)}, bf16[32,3072]{1,0:T(8,128)(2,1)S(1)}, u32[]{:S(2)}, u32[]{:S(2)}) %collective-permute-start.42) | collective-permute-done | bytes 196640 | tf_op jit(solution)/shard_map/ppermute | solution.py:215
  136.4 3.6 %collective-permute-start.49 = (bf16[32,3072]{1,0:T(8,128)(2,1)S(1)}, bf16[32,3072]{1,0:T(8,128)(2,1)S(1)}, u32[]{:S(2)}, u32[]{:S(2)}) collective-permute-start(bf16[32,3072]{1,0:T(8,128)(2,1)S(1)} %get-tuple-element.264), channel_id=1, source_target_pairs={{0,4},{12,8},{1,5},{13,9},{2,6},{14,10},{3,7},{15,11},{16,20},{28,... | collective-permute-start | bytes 589832 | tf_op jit(solution)/shard_map/ppermute | solution.py:215
  140.7 2.4 %collective-permute-start.48 = (bf16[32,3072]{1,0:T(8,128)(2,1)S(1)}, bf16[32,3072]{1,0:T(8,128)(2,1)S(1)}, u32[]{:S(2)}, u32[]{:S(2)}) collective-permute-start(bf16[32,3072]{1,0:T(8,128)(2,1)S(1)} %get-tuple-element.265), channel_id=1, source_target_pairs={{0,4},{4,0},{8,12},{12,8},{1,5},{5,1},{9,13},{13,9},{2,6},{6,2},{1... | collective-permute-start | bytes 589832 | tf_op jit(solution)/shard_map/ppermute | solution.py:215
  143.1 3.2 %collective-permute-done.52.z3 = bf16[48,3072]{1,0:T(8,128)(2,1)S(1)} collective-permute-done((bf16[48,3072]{1,0:T(8,128)(2,1)S(1)}, bf16[48,3072]{1,0:T(8,128)(2,1)S(1)}, u32[]{:S(2)}, u32[]{:S(2)}) %collective-permute-start.52) | collective-permute-done | bytes 294944 | tf_op jit(solution)/shard_map/ppermute | solution.py:215
  147.3 1.7 %collective-permute-start.53 = (bf16[32,3072]{1,0:T(8,128)(2,1)S(1)}, bf16[32,3072]{1,0:T(8,128)(2,1)S(1)}, u32[]{:S(2)}, u32[]{:S(2)}) collective-permute-start(bf16[32,3072]{1,0:T(8,128)(2,1)S(1)} %add_convert_fusion.2), channel_id=1, source_target_pairs={{0,8},{8,0},{4,12},{12,4},{1,9},{9,1},{5,13},{13,5},{2,10},{10,2},... | collective-permute-start | bytes 589832 | tf_op jit(solution)/shard_map/ppermute | solution.py:215
  149.0 1.6 collective-permute-done.48.z2
  150.6 8.7 %collective-permute-done.53.z3 = bf16[32,3072]{1,0:T(8,128)(2,1)S(1)} collective-permute-done((bf16[32,3072]{1,0:T(8,128)(2,1)S(1)}, bf16[32,3072]{1,0:T(8,128)(2,1)S(1)}, u32[]{:S(2)}, u32[]{:S(2)}) %collective-permute-start.53) | collective-permute-done | bytes 196640 | tf_op jit(solution)/shard_map/ppermute | solution.py:215
  (126 shorter events, 41.5 us)
Async XLA Ops:
  1.0 18.3 %collective-permute-start = (bf16[48,3072]{1,0:T(8,128)(2,1)S(1)}, bf16[48,3072]{1,0:T(8,128)(2,1)S(1)}, u32[]{:S(2)}, u32[]{:S(2)}) collective-permute-start(bf16[48,3072]{1,0:T(8,128)(2,1)S(1)} %slice.49.own.x), channel_id=1, source_target_pairs={{0,8},{8,0},{4,12},{12,4},{1,9},{9,1},{5,13},{13,5},{2,10},{10,2},... | collective-permute-start | bytes 884744 | tf_op jit(solution)/shard_map/ppermute | solution.py:215
  5.1 23.8 %collective-permute-start.2 = (bf16[48,3072]{1,0:T(8,128)(2,1)S(1)}, bf16[48,3072]{1,0:T(8,128)(2,1)S(1)}, u32[]{:S(2)}, u32[]{:S(2)}) collective-permute-start(bf16[48,3072]{1,0:T(8,128)(2,1)S(1)} %slice.49.own.x), channel_id=1, source_target_pairs={{0,4},{4,0},{8,12},{12,8},{1,5},{5,1},{9,13},{13,9},{2,6},{6,2},{1... | collective-permute-start | bytes 884744 | tf_op jit(solution)/shard_map/ppermute | solution.py:215
  6.7 22.2 %collective-permute-start.3 = (bf16[48,3072]{1,0:T(8,128)(2,1)S(1)}, bf16[48,3072]{1,0:T(8,128)(2,1)S(1)}, u32[]{:S(2)}, u32[]{:S(2)}) collective-permute-start(bf16[48,3072]{1,0:T(8,128)(2,1)S(1)} %slice.49.own.x), channel_id=1, source_target_pairs={{4,8},{8,4},{5,9},{9,5},{6,10},{10,6},{7,11},{11,7},{20,24},{24,20... | collective-permute-start | bytes 884744 | tf_op jit(solution)/shard_map/ppermute | solution.py:215
  19.3 9.6 %collective-permute-start.4 = (bf16[48,3072]{1,0:T(8,128)(2,1)S(1)}, bf16[48,3072]{1,0:T(8,128)(2,1)S(1)}, u32[]{:S(2)}, u32[]{:S(2)}) collective-permute-start(bf16[48,3072]{1,0:T(8,128)(2,1)S(1)} %collective-permute-done.far), channel_id=1, source_target_pairs={{4,0},{8,12},{5,1},{9,13},{6,2},{10,14},{7,3},{11,15},{20,16},{24,... | collective-permute-start | bytes 884744 | tf_op jit(solution)/shard_map/ppermute | solution.py:215
  20.6 16.9 %collective-permute-start.1 = (bf16[48,3072]{1,0:T(8,128)(2,1)S(1)}, bf16[48,3072]{1,0:T(8,128)(2,1)S(1)}, u32[]{:S(2)}, u32[]{:S(2)}) collective-permute-start(bf16[48,3072]{1,0:T(8,128)(2,1)S(1)} %slice.51.own.x), channel_id=1, source_target_pairs={{0,8},{8,0},{4,12},{12,4},{1,9},{9,1},{5,13},{13,5},{2,10},{10,2},... | collective-permute-start | bytes 884744 | tf_op jit(solution)/shard_map/ppermute | solution.py:215
  30.8 7.3 %collective-permute-start.11 = (bf16[48,3072]{1,0:T(8,128)(2,1)S(1)}, bf16[48,3072]{1,0:T(8,128)(2,1)S(1)}, u32[]{:S(2)}, u32[]{:S(2)}) collective-permute-start(bf16[48,3072]{1,0:T(8,128)(2,1)S(1)} %get-tuple-element.162), channel_id=1, source_target_pairs={{0,1},{1,0},{2,3},{3,2},{4,5},{5,4},{6,7},{7,6},{8,9},{9,8},{10,11... | collective-permute-start | bytes 884744 | tf_op jit(solution)/shard_map/ppermute | solution.py:215
  30.9 9.9 %collective-permute-start.12 = (bf16[48,3072]{1,0:T(8,128)(2,1)S(1)}, bf16[48,3072]{1,0:T(8,128)(2,1)S(1)}, u32[]{:S(2)}, u32[]{:S(2)}) collective-permute-start(bf16[48,3072]{1,0:T(8,128)(2,1)S(1)} %get-tuple-element.167), channel_id=1, source_target_pairs={{0,2},{2,0},{1,3},{3,1},{4,6},{6,4},{5,7},{7,5},{8,10},{10,8},{9,1... | collective-permute-start | bytes 884744 | tf_op jit(solution)/shard_map/ppermute | solution.py:215
  32.5 13.7 %collective-permute-start.13 = (bf16[48,3072]{1,0:T(8,128)(2,1)S(1)}, bf16[48,3072]{1,0:T(8,128)(2,1)S(1)}, u32[]{:S(2)}, u32[]{:S(2)}) collective-permute-start(bf16[48,3072]{1,0:T(8,128)(2,1)S(1)} %get-tuple-element.168), channel_id=1, source_target_pairs={{0,3},{3,0},{1,2},{2,1},{4,7},{7,4},{5,6},{6,5},{8,11},{11,8},{9,1... | collective-permute-start | bytes 884744 | tf_op jit(solution)/shard_map/ppermute | solution.py:215
  32.7 18.1 %collective-permute-start.8 = (bf16[48,3072]{1,0:T(8,128)(2,1)S(1)}, bf16[48,3072]{1,0:T(8,128)(2,1)S(1)}, u32[]{:S(2)}, u32[]{:S(2)}) collective-permute-start(bf16[48,3072]{1,0:T(8,128)(2,1)S(1)} %slice.51.own.x), channel_id=1, source_target_pairs={{0,4},{4,0},{8,12},{12,8},{1,5},{5,1},{9,13},{13,9},{2,6},{6,2},{1... | collective-permute-start | bytes 884744 | tf_op jit(solution)/shard_map/ppermute | solution.py:215
  37.5 16.4 %collective-permute-start.9 = (bf16[48,3072]{1,0:T(8,128)(2,1)S(1)}, bf16[48,3072]{1,0:T(8,128)(2,1)S(1)}, u32[]{:S(2)}, u32[]{:S(2)}) collective-permute-start(bf16[48,3072]{1,0:T(8,128)(2,1)S(1)} %slice.51.own.x), channel_id=1, source_target_pairs={{4,8},{8,4},{5,9},{9,5},{6,10},{10,6},{7,11},{11,7},{20,24},{24,20... | collective-permute-start | bytes 884744 | tf_op jit(solution)/shard_map/ppermute | solution.py:215
  38.2 15.7 %collective-permute-start.10 = (bf16[48,3072]{1,0:T(8,128)(2,1)S(1)}, bf16[48,3072]{1,0:T(8,128)(2,1)S(1)}, u32[]{:S(2)}, u32[]{:S(2)}) collective-permute-start(bf16[48,3072]{1,0:T(8,128)(2,1)S(1)} %collective-permute-done.1.far), channel_id=1, source_target_pairs={{4,0},{8,12},{5,1},{9,13},{6,2},{10,14},{7,3},{11,15},{20,16},{24,... | collective-permute-start | bytes 884744 | tf_op jit(solution)/shard_map/ppermute | solution.py:215
  40.8 16.1 %collective-permute-start.6 = (bf16[32,3072]{1,0:T(8,128)(2,1)S(1)}, bf16[32,3072]{1,0:T(8,128)(2,1)S(1)}, u32[]{:S(2)}, u32[]{:S(2)}) collective-permute-start(bf16[32,3072]{1,0:T(8,128)(2,1)S(1)} %slice.50.own.x), channel_id=1, source_target_pairs={{0,8},{8,0},{4,12},{12,4},{1,9},{9,1},{5,13},{13,5},{2,10},{10,2},... | collective-permute-start | bytes 589832 | tf_op jit(solution)/shard_map/ppermute | solution.py:215
  49.3 9.5 %collective-permute-start.18 = (bf16[96,512]{1,0:T(8,128)(2,1)S(1)}, bf16[96,512]{1,0:T(8,128)(2,1)S(1)}, u32[]{:S(2)}, u32[]{:S(2)}) collective-permute-start(bf16[96,512]{1,0:T(8,128)(2,1)S(1)} %get-tuple-element.184), channel_id=1, source_target_pairs={{0,2},{2,0},{1,3},{3,1},{4,6},{6,4},{5,7},{7,5},{8,10},{10,8},{9,1... | collective-permute-start | bytes 294920 | tf_op jit(solution)/shard_map/ppermute | solution.py:215
  50.9 14.0 %collective-permute-start.5 = (bf16[32,3072]{1,0:T(8,128)(2,1)S(1)}, bf16[32,3072]{1,0:T(8,128)(2,1)S(1)}, u32[]{:S(2)}, u32[]{:S(2)}) collective-permute-start(bf16[32,3072]{1,0:T(8,128)(2,1)S(1)} %slice.50.own.x), channel_id=1, source_target_pairs={{0,4},{4,0},{8,12},{12,8},{1,5},{5,1},{9,13},{13,9},{2,6},{6,2},{1... | collective-permute-start | bytes 589832 | tf_op jit(solution)/shard_map/ppermute | solution.py:215
  56.9 6.2 %collective-permute-start.17 = (bf16[48,3072]{1,0:T(8,128)(2,1)S(1)}, bf16[48,3072]{1,0:T(8,128)(2,1)S(1)}, u32[]{:S(2)}, u32[]{:S(2)}) collective-permute-start(bf16[48,3072]{1,0:T(8,128)(2,1)S(1)} %get-tuple-element.183), channel_id=1, source_target_pairs={{0,1},{1,0},{2,3},{3,2},{4,5},{5,4},{6,7},{7,6},{8,9},{9,8},{10,11... | collective-permute-start | bytes 884744 | tf_op jit(solution)/shard_map/ppermute | solution.py:215
  56.9 9.8 %collective-permute-start.20 = (bf16[48,3072]{1,0:T(8,128)(2,1)S(1)}, bf16[48,3072]{1,0:T(8,128)(2,1)S(1)}, u32[]{:S(2)}, u32[]{:S(2)}) collective-permute-start(bf16[48,3072]{1,0:T(8,128)(2,1)S(1)} %get-tuple-element.194), channel_id=1, source_target_pairs={{0,2},{2,0},{1,3},{3,1},{4,6},{6,4},{5,7},{7,5},{8,10},{10,8},{9,1... | collective-permute-start | bytes 884744 | tf_op jit(solution)/shard_map/ppermute | solution.py:215
  58.4 13.9 %collective-permute-start.21 = (bf16[48,3072]{1,0:T(8,128)(2,1)S(1)}, bf16[48,3072]{1,0:T(8,128)(2,1)S(1)}, u32[]{:S(2)}, u32[]{:S(2)}) collective-permute-start(bf16[48,3072]{1,0:T(8,128)(2,1)S(1)} %get-tuple-element.195), channel_id=1, source_target_pairs={{0,3},{3,0},{1,2},{2,1},{4,7},{7,4},{5,6},{6,5},{8,11},{11,8},{9,1... | collective-permute-start | bytes 884744 | tf_op jit(solution)/shard_map/ppermute | solution.py:215
  64.3 9.8 %collective-permute-start.22 = (bf16[48,512]{1,0:T(8,128)(2,1)S(1)}, bf16[48,512]{1,0:T(8,128)(2,1)S(1)}, u32[]{:S(2)}, u32[]{:S(2)}) collective-permute-start(bf16[48,512]{1,0:T(8,128)(2,1)S(1)} %get-tuple-element.199), channel_id=1, source_target_pairs={{0,1},{1,0},{2,3},{3,2},{4,5},{5,4},{6,7},{7,6},{8,9},{9,8},{10,11... | collective-permute-start | bytes 147464 | tf_op jit(solution)/shard_map/ppermute | solution.py:215
  64.7 21.6 %collective-permute-start.26 = (bf16[48,3072]{1,0:T(8,128)(2,1)S(1)}, bf16[48,3072]{1,0:T(8,128)(2,1)S(1)}, u32[]{:S(2)}, u32[]{:S(2)}) collective-permute-start(bf16[48,3072]{1,0:T(8,128)(2,1)S(1)} %get-tuple-element.210), channel_id=1, source_target_pairs={{0,1},{1,0},{2,3},{3,2},{4,5},{5,4},{6,7},{7,6},{8,9},{9,8},{10,11... | collective-permute-start | bytes 884744 | tf_op jit(solution)/shard_map/ppermute | solution.py:215
  64.9 22.9 %collective-permute-start.27 = (bf16[48,3072]{1,0:T(8,128)(2,1)S(1)}, bf16[48,3072]{1,0:T(8,128)(2,1)S(1)}, u32[]{:S(2)}, u32[]{:S(2)}) collective-permute-start(bf16[48,3072]{1,0:T(8,128)(2,1)S(1)} %get-tuple-element.187), channel_id=1, source_target_pairs={{0,2},{2,0},{1,3},{3,1},{4,6},{6,4},{5,7},{7,5},{8,10},{10,8},{9,1... | collective-permute-start | bytes 884744 | tf_op jit(solution)/shard_map/ppermute | solution.py:215
  66.7 21.4 %collective-permute-start.28 = (bf16[48,3072]{1,0:T(8,128)(2,1)S(1)}, bf16[48,3072]{1,0:T(8,128)(2,1)S(1)}, u32[]{:S(2)}, u32[]{:S(2)}) collective-permute-start(bf16[48,3072]{1,0:T(8,128)(2,1)S(1)} %get-tuple-element.211), channel_id=1, source_target_pairs={{0,3},{3,0},{1,2},{2,1},{4,7},{7,4},{5,6},{6,5},{8,11},{11,8},{9,1... | collective-permute-start | bytes 884744 | tf_op jit(solution)/shard_map/ppermute | solution.py:215
  72.2 4.7 %collective-permute-start.7 = (bf16[32,3072]{1,0:T(8,128)(2,1)S(1)}, bf16[32,3072]{1,0:T(8,128)(2,1)S(1)}, u32[]{:S(2)}, u32[]{:S(2)}) collective-permute-start(bf16[32,3072]{1,0:T(8,128)(2,1)S(1)} %slice.50.own.x), channel_id=1, source_target_pairs={{4,8},{8,4},{5,9},{9,5},{6,10},{10,6},{7,11},{11,7},{20,24},{24,20... | collective-permute-start | bytes 589832 | tf_op jit(solution)/shard_map/ppermute | solution.py:215
  75.6 9.1 %collective-permute-start.16 = (bf16[32,3072]{1,0:T(8,128)(2,1)S(1)}, bf16[32,3072]{1,0:T(8,128)(2,1)S(1)}, u32[]{:S(2)}, u32[]{:S(2)}) collective-permute-start(bf16[32,3072]{1,0:T(8,128)(2,1)S(1)} %collective-permute-done.6.far), channel_id=1, source_target_pairs={{4,0},{8,12},{5,1},{9,13},{6,2},{10,14},{7,3},{11,15},{20,16},{24,... | collective-permute-start | bytes 589832 | tf_op jit(solution)/shard_map/ppermute | solution.py:215
  77.0 11.9 %collective-permute-start.25 = (bf16[96,512]{1,0:T(8,128)(2,1)S(1)}, bf16[96,512]{1,0:T(8,128)(2,1)S(1)}, u32[]{:S(2)}, u32[]{:S(2)}) collective-permute-start(bf16[96,512]{1,0:T(8,128)(2,1)S(1)} %get-tuple-element.209), channel_id=1, source_target_pairs={{0,2},{2,0},{1,3},{3,1},{4,6},{6,4},{5,7},{7,5},{8,10},{10,8},{9,1... | collective-permute-start | bytes 294920 | tf_op jit(solution)/shard_map/ppermute | solution.py:215
  86.2 7.8 %collective-permute-start.24 = (bf16[32,3072]{1,0:T(8,128)(2,1)S(1)}, bf16[32,3072]{1,0:T(8,128)(2,1)S(1)}, u32[]{:S(2)}, u32[]{:S(2)}) collective-permute-start(bf16[32,3072]{1,0:T(8,128)(2,1)S(1)} %get-tuple-element.208), channel_id=1, source_target_pairs={{0,1},{1,0},{2,3},{3,2},{4,5},{5,4},{6,7},{7,6},{8,9},{9,8},{10,11... | collective-permute-start | bytes 589832 | tf_op jit(solution)/shard_map/ppermute | solution.py:215
  86.3 8.9 %collective-permute-start.30 = (bf16[32,3072]{1,0:T(8,128)(2,1)S(1)}, bf16[32,3072]{1,0:T(8,128)(2,1)S(1)}, u32[]{:S(2)}, u32[]{:S(2)}) collective-permute-start(bf16[32,3072]{1,0:T(8,128)(2,1)S(1)} %get-tuple-element.225), channel_id=1, source_target_pairs={{0,2},{2,0},{1,3},{3,1},{4,6},{6,4},{5,7},{7,5},{8,10},{10,8},{9,1... | collective-permute-start | bytes 589832 | tf_op jit(solution)/shard_map/ppermute | solution.py:215
  87.8 9.6 %collective-permute-start.31 = (bf16[32,3072]{1,0:T(8,128)(2,1)S(1)}, bf16[32,3072]{1,0:T(8,128)(2,1)S(1)}, u32[]{:S(2)}, u32[]{:S(2)}) collective-permute-start(bf16[32,3072]{1,0:T(8,128)(2,1)S(1)} %get-tuple-element.226), channel_id=1, source_target_pairs={{0,3},{3,0},{1,2},{2,1},{4,7},{7,4},{5,6},{6,5},{8,11},{11,8},{9,1... | collective-permute-start | bytes 589832 | tf_op jit(solution)/shard_map/ppermute | solution.py:215
  89.9 12.1 %collective-permute-start.38 = (bf16[48,3072]{1,0:T(8,128)(2,1)S(1)}, bf16[48,3072]{1,0:T(8,128)(2,1)S(1)}, u32[]{:S(2)}, u32[]{:S(2)}) collective-permute-start(bf16[48,3072]{1,0:T(8,128)(2,1)S(1)} %get-tuple-element.237), channel_id=1, source_target_pairs={{0,4},{12,8},{1,5},{13,9},{2,6},{14,10},{3,7},{15,11},{16,20},{28,... | collective-permute-start | bytes 884744 | tf_op jit(solution)/shard_map/ppermute | solution.py:215
  97.3 3.9 %collective-permute-start.32 = (bf16[32,512]{1,0:T(8,128)(2,1)S(1)}, bf16[32,512]{1,0:T(8,128)(2,1)S(1)}, u32[]{:S(2)}, u32[]{:S(2)}) collective-permute-start(bf16[32,512]{1,0:T(8,128)(2,1)S(1)} %get-tuple-element.230), channel_id=1, source_target_pairs={{0,1},{1,0},{2,3},{3,2},{4,5},{5,4},{6,7},{7,6},{8,9},{9,8},{10,11... | collective-permute-start | bytes 98312 | tf_op jit(solution)/shard_map/ppermute | solution.py:215
  98.8 2.4 %collective-permute-start.33 = (bf16[32,512]{1,0:T(8,128)(2,1)S(1)}, bf16[32,512]{1,0:T(8,128)(2,1)S(1)}, u32[]{:S(2)}, u32[]{:S(2)}) collective-permute-start(bf16[32,512]{1,0:T(8,128)(2,1)S(1)} %get-tuple-element.231), channel_id=1, source_target_pairs={{0,1},{1,0},{2,3},{3,2},{4,5},{5,4},{6,7},{7,6},{8,9},{9,8},{10,11... | collective-permute-start | bytes 98312 | tf_op jit(solution)/shard_map/ppermute | solution.py:215
  99.0 24.6 %collective-permute-start.44 = (bf16[48,3072]{1,0:T(8,128)(2,1)S(1)}, bf16[48,3072]{1,0:T(8,128)(2,1)S(1)}, u32[]{:S(2)}, u32[]{:S(2)}) collective-permute-start(bf16[48,3072]{1,0:T(8,128)(2,1)S(1)} %get-tuple-element.237), channel_id=1, source_target_pairs={{4,8},{8,4},{5,9},{9,5},{6,10},{10,6},{7,11},{11,7},{20,24},{24,20... | collective-permute-start | bytes 884744 | tf_op jit(solution)/shard_map/ppermute | solution.py:215
  99.7 9.9 %collective-permute-start.36 = (bf16[48,3072]{1,0:T(8,128)(2,1)S(1)}, bf16[48,3072]{1,0:T(8,128)(2,1)S(1)}, u32[]{:S(2)}, u32[]{:S(2)}) collective-permute-start(bf16[48,3072]{1,0:T(8,128)(2,1)S(1)} %get-tuple-element.218), channel_id=1, source_target_pairs={{0,2},{2,0},{1,3},{3,1},{4,6},{6,4},{5,7},{7,5},{8,10},{10,8},{9,1... | collective-permute-start | bytes 884744 | tf_op jit(solution)/shard_map/ppermute | solution.py:215
  101.2 2.3 %collective-permute-start.35 = (bf16[48,3072]{1,0:T(8,128)(2,1)S(1)}, bf16[48,3072]{1,0:T(8,128)(2,1)S(1)}, u32[]{:S(2)}, u32[]{:S(2)}) collective-permute-start(bf16[48,3072]{1,0:T(8,128)(2,1)S(1)} %get-tuple-element.234), channel_id=1, source_target_pairs={{0,1},{1,0},{2,3},{3,2},{4,5},{5,4},{6,7},{7,6},{8,9},{9,8},{10,11... | collective-permute-start | bytes 884744 | tf_op jit(solution)/shard_map/ppermute | solution.py:215
  101.2 13.7 %collective-permute-start.37 = (bf16[48,3072]{1,0:T(8,128)(2,1)S(1)}, bf16[48,3072]{1,0:T(8,128)(2,1)S(1)}, u32[]{:S(2)}, u32[]{:S(2)}) collective-permute-start(bf16[48,3072]{1,0:T(8,128)(2,1)S(1)} %get-tuple-element.235), channel_id=1, source_target_pairs={{0,3},{3,0},{1,2},{2,1},{4,7},{7,4},{5,6},{6,5},{8,11},{11,8},{9,1... | collective-permute-start | bytes 884744 | tf_op jit(solution)/shard_map/ppermute | solution.py:215
  101.9 14.7 %collective-permute-start.34 = (bf16[64,512]{1,0:T(8,128)(2,1)S(1)}, bf16[64,512]{1,0:T(8,128)(2,1)S(1)}, u32[]{:S(2)}, u32[]{:S(2)}) collective-permute-start(bf16[64,512]{1,0:T(8,128)(2,1)S(1)} %get-tuple-element.233), channel_id=1, source_target_pairs={{0,2},{2,0},{1,3},{3,1},{4,6},{6,4},{5,7},{7,5},{8,10},{10,8},{9,1... | collective-permute-start | bytes 196616 | tf_op jit(solution)/shard_map/ppermute | solution.py:215
  103.5 22.5 %collective-permute-start.45 = (bf16[48,3072]{1,0:T(8,128)(2,1)S(1)}, bf16[48,3072]{1,0:T(8,128)(2,1)S(1)}, u32[]{:S(2)}, u32[]{:S(2)}) collective-permute-start(bf16[48,3072]{1,0:T(8,128)(2,1)S(1)} %get-tuple-element.253), channel_id=1, source_target_pairs={{0,4},{4,0},{8,12},{12,8},{1,5},{5,1},{9,13},{13,9},{2,6},{6,2},{1... | collective-permute-start | bytes 884744 | tf_op jit(solution)/shard_map/ppermute | solution.py:215
  109.6 17.8 %collective-permute-start.46 = (bf16[48,3072]{1,0:T(8,128)(2,1)S(1)}, bf16[48,3072]{1,0:T(8,128)(2,1)S(1)}, u32[]{:S(2)}, u32[]{:S(2)}) collective-permute-start(bf16[48,3072]{1,0:T(8,128)(2,1)S(1)} %add_convert_fusion.1), channel_id=1, source_target_pairs={{0,8},{8,0},{4,12},{12,4},{1,9},{9,1},{5,13},{13,5},{2,10},{10,2},... | collective-permute-start | bytes 884744 | tf_op jit(solution)/shard_map/ppermute | solution.py:215
  117.3 3.2 %collective-permute-start.39 = (bf16[64,512]{1,0:T(8,128)(2,1)S(1)}, bf16[64,512]{1,0:T(8,128)(2,1)S(1)}, u32[]{:S(2)}, u32[]{:S(2)}) collective-permute-start(bf16[64,512]{1,0:T(8,128)(2,1)S(1)} %shard_map.113), channel_id=1, source_target_pairs={{0,1},{1,0},{2,3},{3,2},{4,5},{5,4},{6,7},{7,6},{8,9},{9,8},{10,11... | collective-permute-start | bytes 196616 | tf_op jit(solution)/shard_map/ppermute | solution.py:215
  117.4 11.0 %collective-permute-start.43 = (bf16[48,3072]{1,0:T(8,128)(2,1)S(1)}, bf16[48,3072]{1,0:T(8,128)(2,1)S(1)}, u32[]{:S(2)}, u32[]{:S(2)}) collective-permute-start(bf16[48,3072]{1,0:T(8,128)(2,1)S(1)} %get-tuple-element.252), channel_id=1, source_target_pairs={{0,4},{12,8},{1,5},{13,9},{2,6},{14,10},{3,7},{15,11},{16,20},{28,... | collective-permute-start | bytes 884744 | tf_op jit(solution)/shard_map/ppermute | solution.py:215
  120.5 20.2 %collective-permute-start.50 = (bf16[48,3072]{1,0:T(8,128)(2,1)S(1)}, bf16[48,3072]{1,0:T(8,128)(2,1)S(1)}, u32[]{:S(2)}, u32[]{:S(2)}) collective-permute-start(bf16[48,3072]{1,0:T(8,128)(2,1)S(1)} %get-tuple-element.252), channel_id=1, source_target_pairs={{4,8},{8,4},{5,9},{9,5},{6,10},{10,6},{7,11},{11,7},{20,24},{24,20... | collective-permute-start | bytes 884744 | tf_op jit(solution)/shard_map/ppermute | solution.py:215
  123.6 19.5 %collective-permute-start.51 = (bf16[48,3072]{1,0:T(8,128)(2,1)S(1)}, bf16[48,3072]{1,0:T(8,128)(2,1)S(1)}, u32[]{:S(2)}, u32[]{:S(2)}) collective-permute-start(bf16[48,3072]{1,0:T(8,128)(2,1)S(1)} %get-tuple-element.267), channel_id=1, source_target_pairs={{0,4},{4,0},{8,12},{12,8},{1,5},{5,1},{9,13},{13,9},{2,6},{6,2},{1... | collective-permute-start | bytes 884744 | tf_op jit(solution)/shard_map/ppermute | solution.py:215
  126.0 7.7 %collective-permute-start.41 = (bf16[32,3072]{1,0:T(8,128)(2,1)S(1)}, bf16[32,3072]{1,0:T(8,128)(2,1)S(1)}, u32[]{:S(2)}, u32[]{:S(2)}) collective-permute-start(bf16[32,3072]{1,0:T(8,128)(2,1)S(1)} %get-tuple-element.245), channel_id=1, source_target_pairs={{0,2},{2,0},{1,3},{3,1},{4,6},{6,4},{5,7},{7,5},{8,10},{10,8},{9,1... | collective-permute-start | bytes 589832 | tf_op jit(solution)/shard_map/ppermute | solution.py:215
  128.4 7.4 %collective-permute-start.42 = (bf16[32,3072]{1,0:T(8,128)(2,1)S(1)}, bf16[32,3072]{1,0:T(8,128)(2,1)S(1)}, u32[]{:S(2)}, u32[]{:S(2)}) collective-permute-start(bf16[32,3072]{1,0:T(8,128)(2,1)S(1)} %get-tuple-element.250), channel_id=1, source_target_pairs={{0,3},{3,0},{1,2},{2,1},{4,7},{7,4},{5,6},{6,5},{8,11},{11,8},{9,1... | collective-permute-start | bytes 589832 | tf_op jit(solution)/shard_map/ppermute | solution.py:215
  129.3 17.1 %collective-permute-start.52 = (bf16[48,3072]{1,0:T(8,128)(2,1)S(1)}, bf16[48,3072]{1,0:T(8,128)(2,1)S(1)}, u32[]{:S(2)}, u32[]{:S(2)}) collective-permute-start(bf16[48,3072]{1,0:T(8,128)(2,1)S(1)} %add_convert_fusion), channel_id=1, source_target_pairs={{0,8},{8,0},{4,12},{12,4},{1,9},{9,1},{5,13},{13,5},{2,10},{10,2},... | collective-permute-start | bytes 884744 | tf_op jit(solution)/shard_map/ppermute | solution.py:215
  136.4 10.9 %collective-permute-start.49 = (bf16[32,3072]{1,0:T(8,128)(2,1)S(1)}, bf16[32,3072]{1,0:T(8,128)(2,1)S(1)}, u32[]{:S(2)}, u32[]{:S(2)}) collective-permute-start(bf16[32,3072]{1,0:T(8,128)(2,1)S(1)} %get-tuple-element.264), channel_id=1, source_target_pairs={{0,4},{12,8},{1,5},{13,9},{2,6},{14,10},{3,7},{15,11},{16,20},{28,... | collective-permute-start | bytes 589832 | tf_op jit(solution)/shard_map/ppermute | solution.py:215
  140.0 9.0 %collective-permute-start.47 = (bf16[32,3072]{1,0:T(8,128)(2,1)S(1)}, bf16[32,3072]{1,0:T(8,128)(2,1)S(1)}, u32[]{:S(2)}, u32[]{:S(2)}) collective-permute-start(bf16[32,3072]{1,0:T(8,128)(2,1)S(1)} %get-tuple-element.264), channel_id=1, source_target_pairs={{4,8},{8,4},{5,9},{9,5},{6,10},{10,6},{7,11},{11,7},{20,24},{24,20... | collective-permute-start | bytes 589832 | tf_op jit(solution)/shard_map/ppermute | solution.py:215
  140.7 9.9 %collective-permute-start.48 = (bf16[32,3072]{1,0:T(8,128)(2,1)S(1)}, bf16[32,3072]{1,0:T(8,128)(2,1)S(1)}, u32[]{:S(2)}, u32[]{:S(2)}) collective-permute-start(bf16[32,3072]{1,0:T(8,128)(2,1)S(1)} %get-tuple-element.265), channel_id=1, source_target_pairs={{0,4},{4,0},{8,12},{12,8},{1,5},{5,1},{9,13},{13,9},{2,6},{6,2},{1... | collective-permute-start | bytes 589832 | tf_op jit(solution)/shard_map/ppermute | solution.py:215
  147.3 12.0 %collective-permute-start.53 = (bf16[32,3072]{1,0:T(8,128)(2,1)S(1)}, bf16[32,3072]{1,0:T(8,128)(2,1)S(1)}, u32[]{:S(2)}, u32[]{:S(2)}) collective-permute-start(bf16[32,3072]{1,0:T(8,128)(2,1)S(1)} %add_convert_fusion.2), channel_id=1, source_target_pairs={{0,8},{8,0},{4,12},{12,4},{1,9},{9,1},{5,13},{13,5},{2,10},{10,2},... | collective-permute-start | bytes 589832 | tf_op jit(solution)/shard_map/ppermute | solution.py:215
  (7 other events, 17.0 us)

commit v3 on v2

--- a/solution.py
+++ b/solution.py
@@ -12,7 +12,7 @@
 PIECES = (3, 3, 2)
 DIRECT_IN = ()
 MID_LATE = ()
-NEAR_LATE = ()
+NEAR_LATE = (0, 1)
 DIRECT_OUT = ()
 ORDER = (
     "Z0 P W0 Z1",

time: 161 us -> 161 us (level)
  transfers between devices with their start and end apart: 54 -> 54, of which waited for: 20 -> 23; matrix products, arithmetic and copies ran while one was open for 4% -> 4% of each run, Pallas kernels for 21% -> 21%
where the time goes in v3:
time: 161 us; the launch traced here: 160 us
  starting transfers between devices  69 us (43%)
  waiting for transfers between devices  48.2 us (30%)
  Pallas kernels  34.4 us (21%)
  other arithmetic  4.58 us (3%)
  local copies, waits for them, and re-layouts  2.94 us (2%)
    ppermute x54, starting transfers between devices, swap(): return lax.ppermute(x, axis, pairs)  69 us
    ppermute x54, waiting for transfers between devices, swap(): return lax.ppermute(x, axis, pairs)  48.2 us
    pallas_call x12, Pallas kernels, product(): call(functools.partial(product_kernel, n), [jax.ShapeDtypeStruct((rows, w...  14.1 us
    pallas_call x2, Pallas kernels, pack(): call(functools.partial(pack_kernel, groups, rows_packed), outs, [SMEM, SM...  8.45 us
    pallas_call x3, Pallas kernels, normalize(): call(functools.partial(norm_kernel, len(parts) - 3), [out] * 4, [SMEM] +...  5.22 us
  transfers between devices with their start and end apart: 54, of which 23 were waited for; matrix products, arithmetic and copies ran while one was open for 4% of the time, Pallas kernels for 21%

profile of v3, /device:TPU:0, one launch (start us, length us, event | category | flops | bytes accessed | tf_op | source)
XLA Modules:
  0.0 159.9 jit_solution(11854322869693198228)
XLA Ops:
  1.0 4.1 %collective-permute-start = (bf16[48,3072]{1,0:T(8,128)(2,1)S(1)}, bf16[48,3072]{1,0:T(8,128)(2,1)S(1)}, u32[]{:S(2)}, u32[]{:S(2)}) collective-permute-start(bf16[48,3072]{1,0:T(8,128)(2,1)S(1)} %slice.49.own.x), channel_id=1, source_target_pairs={{0,8},{8,0},{4,12},{12,4},{1,9},{9,1},{5,13},{13,5},{2,10},{10,2},... | collective-permute-start | bytes 884744 | tf_op jit(solution)/shard_map/ppermute | solution.py:215
  5.1 1.6 collective-permute-start.2
  13.5 4.5 %shard_map.91 = (bf16[2,3072,512]{2,1,0:T(8,128)(2,1)S(1)}, bf16[2,3072,512]{2,1,0:T(8,128)(2,1)S(1)}) custom-call(s32[4,4]{1,0:T(4,128)S(1)} %broadcast_select_fusion.1.sid, s32[4]{0:T(128)S(1)} %broadcast_select_fusion.2.live, bf16[3072,6144]{1,0:T(8,128)(2,1)} %w.2), custom_call_target="tpu_custom_call" | custom-call | tf_op jit(solution)/shard_map/pallas_call | solution.py:147
  19.3 1.3 collective-permute-start.4
  20.6 4.0 %collective-permute-start.1 = (bf16[48,3072]{1,0:T(8,128)(2,1)S(1)}, bf16[48,3072]{1,0:T(8,128)(2,1)S(1)}, u32[]{:S(2)}, u32[]{:S(2)}) collective-permute-start(bf16[48,3072]{1,0:T(8,128)(2,1)S(1)} %slice.51.own.x), channel_id=1, source_target_pairs={{0,8},{8,0},{4,12},{12,4},{1,9},{9,1},{5,13},{13,5},{2,10},{10,2},... | collective-permute-start | bytes 884744 | tf_op jit(solution)/shard_map/ppermute | solution.py:215
  24.6 4.0 %shard_map.92 = (bf16[2,512,3072]{2,1,0:T(8,128)(2,1)S(1)}, bf16[2,512,3072]{2,1,0:T(8,128)(2,1)S(1)}) custom-call(s32[4,4]{1,0:T(4,128)S(1)} %broadcast_select_fusion.1.sid, s32[4]{0:T(128)S(1)} %broadcast_select_fusion.2.live, bf16[6144,3072]{1,0:T(8,128)(2,1)} %w.3), custom_call_target="tpu_custom_call" | custom-call | tf_op jit(solution)/shard_map/pallas_call | solution.py:147
  28.6 1.9 %shard_map.93 = (bf16[48,3072]{1,0:T(8,128)(2,1)S(1)}, bf16[48,3072]{1,0:T(8,128)(2,1)S(1)}, bf16[48,3072]{1,0:T(8,128)(2,1)S(1)}, bf16[48,3072]{1,0:T(8,128)(2,1)S(1)}) custom-call(s32[2]{0:T(128)S(1)} %pad_add_fusion.where_ref, f32[4,1,3072]{2,1,0:T(1,128)S(1)} %bitcast.12, f32[4,1,3072]{2,1,0:T(1,128)S(1)} %bitcast.15, bf16[48,3072]{1,0:T(8,128)(2,1)S(1)} %slice.49.own.x, ...), custom_call_target="tpu_custom_call" | custom-call | tf_op jit(solution)/shard_map/pallas_call | solution.py:110
  30.6 1.2 collective-permute-start.12
  32.5 3.3 %collective-permute-start.8 = (bf16[48,3072]{1,0:T(8,128)(2,1)S(1)}, bf16[48,3072]{1,0:T(8,128)(2,1)S(1)}, u32[]{:S(2)}, u32[]{:S(2)}) collective-permute-start(bf16[48,3072]{1,0:T(8,128)(2,1)S(1)} %slice.51.own.x), channel_id=1, source_target_pairs={{0,4},{4,0},{8,12},{12,8},{1,5},{5,1},{9,13},{13,9},{2,6},{6,2},{1... | collective-permute-start | bytes 884744 | tf_op jit(solution)/shard_map/ppermute | solution.py:215
  35.8 1.7 %collective-permute-done.1.far = bf16[48,3072]{1,0:T(8,128)(2,1)S(1)} collective-permute-done((bf16[48,3072]{1,0:T(8,128)(2,1)S(1)}, bf16[48,3072]{1,0:T(8,128)(2,1)S(1)}, u32[]{:S(2)}, u32[]{:S(2)}) %collective-permute-start.1) | collective-permute-done | bytes 294944 | tf_op jit(solution)/shard_map/ppermute | solution.py:215
  38.2 1.3 collective-permute-start.10
  40.5 3.8 %collective-permute-start.6 = (bf16[32,3072]{1,0:T(8,128)(2,1)S(1)}, bf16[32,3072]{1,0:T(8,128)(2,1)S(1)}, u32[]{:S(2)}, u32[]{:S(2)}) collective-permute-start(bf16[32,3072]{1,0:T(8,128)(2,1)S(1)} %slice.50.own.x), channel_id=1, source_target_pairs={{0,8},{8,0},{4,12},{12,4},{1,9},{9,1},{5,13},{13,5},{2,10},{10,2},... | collective-permute-start | bytes 589832 | tf_op jit(solution)/shard_map/ppermute | solution.py:215
  47.8 1.2 collective-permute-done.15.r3
  49.0 1.2 collective-permute-start.18
  50.2 3.8 %collective-permute-start.5 = (bf16[32,3072]{1,0:T(8,128)(2,1)S(1)}, bf16[32,3072]{1,0:T(8,128)(2,1)S(1)}, u32[]{:S(2)}, u32[]{:S(2)}) collective-permute-start(bf16[32,3072]{1,0:T(8,128)(2,1)S(1)} %slice.50.own.x), channel_id=1, source_target_pairs={{0,4},{4,0},{8,12},{12,8},{1,5},{5,1},{9,13},{13,9},{2,6},{6,2},{1... | collective-permute-start | bytes 589832 | tf_op jit(solution)/shard_map/ppermute | solution.py:215
  54.1 1.9 %shard_map.97 = (bf16[48,3072]{1,0:T(8,128)(2,1)S(1)}, bf16[48,3072]{1,0:T(8,128)(2,1)S(1)}, bf16[48,3072]{1,0:T(8,128)(2,1)S(1)}, bf16[48,3072]{1,0:T(8,128)(2,1)S(1)}) custom-call(s32[2]{0:T(128)S(1)} %pad_add_fusion.where_ref, f32[4,1,3072]{2,1,0:T(1,128)S(1)} %bitcast.13, f32[4,1,3072]{2,1,0:T(1,128)S(1)} %bitcast.16, bf16[48,3072]{1,0:T(8,128)(2,1)S(1)} %slice.51.own.x, ...), custom_call_target="tpu_custom_call" | custom-call | tf_op jit(solution)/shard_map/pallas_call | solution.py:110
  56.9 1.5 collective-permute-start.20
  60.7 1.2 shard_map.99
  61.9 1.2 shard_map.100
  64.9 1.5 collective-permute-start.27
  67.1 5.1 %collective-permute-done.21.refs_1_ = bf16[48,3072]{1,0:T(8,128)(2,1)S(1)} collective-permute-done((bf16[48,3072]{1,0:T(8,128)(2,1)S(1)}, bf16[48,3072]{1,0:T(8,128)(2,1)S(1)}, u32[]{:S(2)}, u32[]{:S(2)}) %collective-permute-start.21) | collective-permute-done | bytes 294944 | tf_op jit(solution)/shard_map/ppermute | solution.py:215
  75.6 1.3 collective-permute-start.16
  77.0 1.6 collective-permute-start.25
  78.5 6.2 %collective-permute-done.16.rest_1_ = bf16[32,3072]{1,0:T(8,128)(2,1)S(1)} collective-permute-done((bf16[32,3072]{1,0:T(8,128)(2,1)S(1)}, bf16[32,3072]{1,0:T(8,128)(2,1)S(1)}, u32[]{:S(2)}, u32[]{:S(2)}) %collective-permute-start.16) | collective-permute-done | bytes 196640 | tf_op jit(solution)/shard_map/ppermute | solution.py:215
  84.7 1.4 shard_map.104
  86.3 1.5 collective-permute-start.30
  89.9 1.6 %collective-permute-start.38 = (bf16[48,3072]{1,0:T(8,128)(2,1)S(1)}, bf16[48,3072]{1,0:T(8,128)(2,1)S(1)}, u32[]{:S(2)}, u32[]{:S(2)}) collective-permute-start(bf16[48,3072]{1,0:T(8,128)(2,1)S(1)} %get-tuple-element.239), channel_id=1, source_target_pairs={{0,4},{12,8},{1,5},{13,9},{2,6},{14,10},{3,7},{15,11},{16,20},{28,... | collective-permute-start | bytes 884744 | tf_op jit(solution)/shard_map/ppermute | solution.py:215
  91.5 1.2 shard_map.107
  92.7 1.2 shard_map.108
  95.1 2.2 %collective-permute-done.31.refs_1_ = bf16[32,3072]{1,0:T(8,128)(2,1)S(1)} collective-permute-done((bf16[32,3072]{1,0:T(8,128)(2,1)S(1)}, bf16[32,3072]{1,0:T(8,128)(2,1)S(1)}, u32[]{:S(2)}, u32[]{:S(2)}) %collective-permute-start.31) | collective-permute-done | bytes 196640 | tf_op jit(solution)/shard_map/ppermute | solution.py:215
  99.7 1.5 collective-permute-start.36
  101.9 1.5 collective-permute-start.34
  103.5 1.2 collective-permute-start.45
  104.7 4.9 %collective-permute-done.36.y2 = bf16[48,3072]{1,0:T(8,128)(2,1)S(1)} collective-permute-done((bf16[48,3072]{1,0:T(8,128)(2,1)S(1)}, bf16[48,3072]{1,0:T(8,128)(2,1)S(1)}, u32[]{:S(2)}, u32[]{:S(2)}) %collective-permute-start.36) | collective-permute-done | bytes 294944 | tf_op jit(solution)/shard_map/ppermute | solution.py:215
  109.6 2.3 %collective-permute-start.46 = (bf16[48,3072]{1,0:T(8,128)(2,1)S(1)}, bf16[48,3072]{1,0:T(8,128)(2,1)S(1)}, u32[]{:S(2)}, u32[]{:S(2)}) collective-permute-start(bf16[48,3072]{1,0:T(8,128)(2,1)S(1)} %add_convert_fusion.1), channel_id=1, source_target_pairs={{0,8},{8,0},{4,12},{12,4},{1,9},{9,1},{5,13},{13,5},{2,10},{10,2},... | collective-permute-start | bytes 884744 | tf_op jit(solution)/shard_map/ppermute | solution.py:215
  111.9 2.9 %collective-permute-done.37.y3 = bf16[48,3072]{1,0:T(8,128)(2,1)S(1)} collective-permute-done((bf16[48,3072]{1,0:T(8,128)(2,1)S(1)}, bf16[48,3072]{1,0:T(8,128)(2,1)S(1)}, u32[]{:S(2)}, u32[]{:S(2)}) %collective-permute-start.37) | collective-permute-done | bytes 294944 | tf_op jit(solution)/shard_map/ppermute | solution.py:215
  117.4 3.1 %collective-permute-start.43 = (bf16[48,3072]{1,0:T(8,128)(2,1)S(1)}, bf16[48,3072]{1,0:T(8,128)(2,1)S(1)}, u32[]{:S(2)}, u32[]{:S(2)}) collective-permute-start(bf16[48,3072]{1,0:T(8,128)(2,1)S(1)} %get-tuple-element.254), channel_id=1, source_target_pairs={{0,4},{12,8},{1,5},{13,9},{2,6},{14,10},{3,7},{15,11},{16,20},{28,... | collective-permute-start | bytes 884744 | tf_op jit(solution)/shard_map/ppermute | solution.py:215
  122.4 1.2 shard_map.115
  123.6 1.5 collective-permute-start.41
  127.2 2.5 %collective-permute-start.51 = (bf16[48,3072]{1,0:T(8,128)(2,1)S(1)}, bf16[48,3072]{1,0:T(8,128)(2,1)S(1)}, u32[]{:S(2)}, u32[]{:S(2)}) collective-permute-start(bf16[48,3072]{1,0:T(8,128)(2,1)S(1)} %get-tuple-element.271), channel_id=1, source_target_pairs={{0,4},{4,0},{8,12},{12,8},{1,5},{5,1},{9,13},{13,9},{2,6},{6,2},{1... | collective-permute-start | bytes 884744 | tf_op jit(solution)/shard_map/ppermute | solution.py:215
  129.8 1.2 collective-permute-start.52
  131.4 2.5 %collective-permute-done.42.y3 = bf16[32,3072]{1,0:T(8,128)(2,1)S(1)} collective-permute-done((bf16[32,3072]{1,0:T(8,128)(2,1)S(1)}, bf16[32,3072]{1,0:T(8,128)(2,1)S(1)}, u32[]{:S(2)}, u32[]{:S(2)}) %collective-permute-start.42) | collective-permute-done | bytes 196640 | tf_op jit(solution)/shard_map/ppermute | solution.py:215
  134.5 4.2 %collective-permute-start.49 = (bf16[32,3072]{1,0:T(8,128)(2,1)S(1)}, bf16[32,3072]{1,0:T(8,128)(2,1)S(1)}, u32[]{:S(2)}, u32[]{:S(2)}) collective-permute-start(bf16[32,3072]{1,0:T(8,128)(2,1)S(1)} %get-tuple-element.267), channel_id=1, source_target_pairs={{0,4},{12,8},{1,5},{13,9},{2,6},{14,10},{3,7},{15,11},{16,20},{28,... | collective-permute-start | bytes 589832 | tf_op jit(solution)/shard_map/ppermute | solution.py:215
  140.5 2.2 %collective-permute-done.51.z2 = bf16[48,3072]{1,0:T(8,128)(2,1)S(1)} collective-permute-done((bf16[48,3072]{1,0:T(8,128)(2,1)S(1)}, bf16[48,3072]{1,0:T(8,128)(2,1)S(1)}, u32[]{:S(2)}, u32[]{:S(2)}) %collective-permute-start.51) | collective-permute-done | bytes 294944 | tf_op jit(solution)/shard_map/ppermute | solution.py:215
  142.7 1.5 collective-permute-done.52.z3
  145.1 2.7 %collective-permute-done.49 = bf16[32,3072]{1,0:T(8,128)(2,1)S(1)} collective-permute-done((bf16[32,3072]{1,0:T(8,128)(2,1)S(1)}, bf16[32,3072]{1,0:T(8,128)(2,1)S(1)}, u32[]{:S(2)}, u32[]{:S(2)}) %collective-permute-start.49) | collective-permute-done | bytes 196640 | tf_op jit(solution)/shard_map/ppermute | solution.py:215
  147.8 3.7 %collective-permute-start.53 = (bf16[32,3072]{1,0:T(8,128)(2,1)S(1)}, bf16[32,3072]{1,0:T(8,128)(2,1)S(1)}, u32[]{:S(2)}, u32[]{:S(2)}) collective-permute-start(bf16[32,3072]{1,0:T(8,128)(2,1)S(1)} %add_convert_fusion.2), channel_id=1, source_target_pairs={{0,8},{8,0},{4,12},{12,4},{1,9},{9,1},{5,13},{13,5},{2,10},{10,2},... | collective-permute-start | bytes 589832 | tf_op jit(solution)/shard_map/ppermute | solution.py:215
  152.0 7.0 %collective-permute-done.53.z3 = bf16[32,3072]{1,0:T(8,128)(2,1)S(1)} collective-permute-done((bf16[32,3072]{1,0:T(8,128)(2,1)S(1)}, bf16[32,3072]{1,0:T(8,128)(2,1)S(1)}, u32[]{:S(2)}, u32[]{:S(2)}) %collective-permute-start.53) | collective-permute-done | bytes 196640 | tf_op jit(solution)/shard_map/ppermute | solution.py:215
  (126 shorter events, 42.1 us)
Async XLA Ops:
  1.0 18.3 %collective-permute-start = (bf16[48,3072]{1,0:T(8,128)(2,1)S(1)}, bf16[48,3072]{1,0:T(8,128)(2,1)S(1)}, u32[]{:S(2)}, u32[]{:S(2)}) collective-permute-start(bf16[48,3072]{1,0:T(8,128)(2,1)S(1)} %slice.49.own.x), channel_id=1, source_target_pairs={{0,8},{8,0},{4,12},{12,4},{1,9},{9,1},{5,13},{13,5},{2,10},{10,2},... | collective-permute-start | bytes 884744 | tf_op jit(solution)/shard_map/ppermute | solution.py:215
  5.1 23.5 %collective-permute-start.2 = (bf16[48,3072]{1,0:T(8,128)(2,1)S(1)}, bf16[48,3072]{1,0:T(8,128)(2,1)S(1)}, u32[]{:S(2)}, u32[]{:S(2)}) collective-permute-start(bf16[48,3072]{1,0:T(8,128)(2,1)S(1)} %slice.49.own.x), channel_id=1, source_target_pairs={{0,4},{4,0},{8,12},{12,8},{1,5},{5,1},{9,13},{13,9},{2,6},{6,2},{1... | collective-permute-start | bytes 884744 | tf_op jit(solution)/shard_map/ppermute | solution.py:215
  6.7 22.0 %collective-permute-start.3 = (bf16[48,3072]{1,0:T(8,128)(2,1)S(1)}, bf16[48,3072]{1,0:T(8,128)(2,1)S(1)}, u32[]{:S(2)}, u32[]{:S(2)}) collective-permute-start(bf16[48,3072]{1,0:T(8,128)(2,1)S(1)} %slice.49.own.x), channel_id=1, source_target_pairs={{4,8},{8,4},{5,9},{9,5},{6,10},{10,6},{7,11},{11,7},{20,24},{24,20... | collective-permute-start | bytes 884744 | tf_op jit(solution)/shard_map/ppermute | solution.py:215
  19.3 9.3 %collective-permute-start.4 = (bf16[48,3072]{1,0:T(8,128)(2,1)S(1)}, bf16[48,3072]{1,0:T(8,128)(2,1)S(1)}, u32[]{:S(2)}, u32[]{:S(2)}) collective-permute-start(bf16[48,3072]{1,0:T(8,128)(2,1)S(1)} %collective-permute-done.far), channel_id=1, source_target_pairs={{4,0},{8,12},{5,1},{9,13},{6,2},{10,14},{7,3},{11,15},{20,16},{24,... | collective-permute-start | bytes 884744 | tf_op jit(solution)/shard_map/ppermute | solution.py:215
  20.6 16.9 %collective-permute-start.1 = (bf16[48,3072]{1,0:T(8,128)(2,1)S(1)}, bf16[48,3072]{1,0:T(8,128)(2,1)S(1)}, u32[]{:S(2)}, u32[]{:S(2)}) collective-permute-start(bf16[48,3072]{1,0:T(8,128)(2,1)S(1)} %slice.51.own.x), channel_id=1, source_target_pairs={{0,8},{8,0},{4,12},{12,4},{1,9},{9,1},{5,13},{13,5},{2,10},{10,2},... | collective-permute-start | bytes 884744 | tf_op jit(solution)/shard_map/ppermute | solution.py:215
  30.5 7.6 %collective-permute-start.11 = (bf16[48,3072]{1,0:T(8,128)(2,1)S(1)}, bf16[48,3072]{1,0:T(8,128)(2,1)S(1)}, u32[]{:S(2)}, u32[]{:S(2)}) collective-permute-start(bf16[48,3072]{1,0:T(8,128)(2,1)S(1)} %get-tuple-element.164), channel_id=1, source_target_pairs={{0,1},{1,0},{2,3},{3,2},{4,5},{5,4},{6,7},{7,6},{8,9},{9,8},{10,11... | collective-permute-start | bytes 884744 | tf_op jit(solution)/shard_map/ppermute | solution.py:215
  30.6 9.9 %collective-permute-start.12 = (bf16[48,3072]{1,0:T(8,128)(2,1)S(1)}, bf16[48,3072]{1,0:T(8,128)(2,1)S(1)}, u32[]{:S(2)}, u32[]{:S(2)}) collective-permute-start(bf16[48,3072]{1,0:T(8,128)(2,1)S(1)} %get-tuple-element.169), channel_id=1, source_target_pairs={{0,2},{2,0},{1,3},{3,1},{4,6},{6,4},{5,7},{7,5},{8,10},{10,8},{9,1... | collective-permute-start | bytes 884744 | tf_op jit(solution)/shard_map/ppermute | solution.py:215
  31.8 14.1 %collective-permute-start.13 = (bf16[48,3072]{1,0:T(8,128)(2,1)S(1)}, bf16[48,3072]{1,0:T(8,128)(2,1)S(1)}, u32[]{:S(2)}, u32[]{:S(2)}) collective-permute-start(bf16[48,3072]{1,0:T(8,128)(2,1)S(1)} %get-tuple-element.170), channel_id=1, source_target_pairs={{0,3},{3,0},{1,2},{2,1},{4,7},{7,4},{5,6},{6,5},{8,11},{11,8},{9,1... | collective-permute-start | bytes 884744 | tf_op jit(solution)/shard_map/ppermute | solution.py:215
  32.5 17.7 %collective-permute-start.8 = (bf16[48,3072]{1,0:T(8,128)(2,1)S(1)}, bf16[48,3072]{1,0:T(8,128)(2,1)S(1)}, u32[]{:S(2)}, u32[]{:S(2)}) collective-permute-start(bf16[48,3072]{1,0:T(8,128)(2,1)S(1)} %slice.51.own.x), channel_id=1, source_target_pairs={{0,4},{4,0},{8,12},{12,8},{1,5},{5,1},{9,13},{13,9},{2,6},{6,2},{1... | collective-permute-start | bytes 884744 | tf_op jit(solution)/shard_map/ppermute | solution.py:215
  37.5 16.6 %collective-permute-start.9 = (bf16[48,3072]{1,0:T(8,128)(2,1)S(1)}, bf16[48,3072]{1,0:T(8,128)(2,1)S(1)}, u32[]{:S(2)}, u32[]{:S(2)}) collective-permute-start(bf16[48,3072]{1,0:T(8,128)(2,1)S(1)} %slice.51.own.x), channel_id=1, source_target_pairs={{4,8},{8,4},{5,9},{9,5},{6,10},{10,6},{7,11},{11,7},{20,24},{24,20... | collective-permute-start | bytes 884744 | tf_op jit(solution)/shard_map/ppermute | solution.py:215
  38.2 15.9 %collective-permute-start.10 = (bf16[48,3072]{1,0:T(8,128)(2,1)S(1)}, bf16[48,3072]{1,0:T(8,128)(2,1)S(1)}, u32[]{:S(2)}, u32[]{:S(2)}) collective-permute-start(bf16[48,3072]{1,0:T(8,128)(2,1)S(1)} %collective-permute-done.1.far), channel_id=1, source_target_pairs={{4,0},{8,12},{5,1},{9,13},{6,2},{10,14},{7,3},{11,15},{20,16},{24,... | collective-permute-start | bytes 884744 | tf_op jit(solution)/shard_map/ppermute | solution.py:215
  40.5 16.4 %collective-permute-start.6 = (bf16[32,3072]{1,0:T(8,128)(2,1)S(1)}, bf16[32,3072]{1,0:T(8,128)(2,1)S(1)}, u32[]{:S(2)}, u32[]{:S(2)}) collective-permute-start(bf16[32,3072]{1,0:T(8,128)(2,1)S(1)} %slice.50.own.x), channel_id=1, source_target_pairs={{0,8},{8,0},{4,12},{12,4},{1,9},{9,1},{5,13},{13,5},{2,10},{10,2},... | collective-permute-start | bytes 589832 | tf_op jit(solution)/shard_map/ppermute | solution.py:215
  49.0 9.7 %collective-permute-start.18 = (bf16[96,512]{1,0:T(8,128)(2,1)S(1)}, bf16[96,512]{1,0:T(8,128)(2,1)S(1)}, u32[]{:S(2)}, u32[]{:S(2)}) collective-permute-start(bf16[96,512]{1,0:T(8,128)(2,1)S(1)} %get-tuple-element.186), channel_id=1, source_target_pairs={{0,2},{2,0},{1,3},{3,1},{4,6},{6,4},{5,7},{7,5},{8,10},{10,8},{9,1... | collective-permute-start | bytes 294920 | tf_op jit(solution)/shard_map/ppermute | solution.py:215
  50.2 14.7 %collective-permute-start.5 = (bf16[32,3072]{1,0:T(8,128)(2,1)S(1)}, bf16[32,3072]{1,0:T(8,128)(2,1)S(1)}, u32[]{:S(2)}, u32[]{:S(2)}) collective-permute-start(bf16[32,3072]{1,0:T(8,128)(2,1)S(1)} %slice.50.own.x), channel_id=1, source_target_pairs={{0,4},{4,0},{8,12},{12,8},{1,5},{5,1},{9,13},{13,9},{2,6},{6,2},{1... | collective-permute-start | bytes 589832 | tf_op jit(solution)/shard_map/ppermute | solution.py:215
  56.9 6.2 %collective-permute-start.17 = (bf16[48,3072]{1,0:T(8,128)(2,1)S(1)}, bf16[48,3072]{1,0:T(8,128)(2,1)S(1)}, u32[]{:S(2)}, u32[]{:S(2)}) collective-permute-start(bf16[48,3072]{1,0:T(8,128)(2,1)S(1)} %get-tuple-element.185), channel_id=1, source_target_pairs={{0,1},{1,0},{2,3},{3,2},{4,5},{5,4},{6,7},{7,6},{8,9},{9,8},{10,11... | collective-permute-start | bytes 884744 | tf_op jit(solution)/shard_map/ppermute | solution.py:215
  56.9 9.8 %collective-permute-start.20 = (bf16[48,3072]{1,0:T(8,128)(2,1)S(1)}, bf16[48,3072]{1,0:T(8,128)(2,1)S(1)}, u32[]{:S(2)}, u32[]{:S(2)}) collective-permute-start(bf16[48,3072]{1,0:T(8,128)(2,1)S(1)} %get-tuple-element.196), channel_id=1, source_target_pairs={{0,2},{2,0},{1,3},{3,1},{4,6},{6,4},{5,7},{7,5},{8,10},{10,8},{9,1... | collective-permute-start | bytes 884744 | tf_op jit(solution)/shard_map/ppermute | solution.py:215
  58.4 13.9 %collective-permute-start.21 = (bf16[48,3072]{1,0:T(8,128)(2,1)S(1)}, bf16[48,3072]{1,0:T(8,128)(2,1)S(1)}, u32[]{:S(2)}, u32[]{:S(2)}) collective-permute-start(bf16[48,3072]{1,0:T(8,128)(2,1)S(1)} %get-tuple-element.197), channel_id=1, source_target_pairs={{0,3},{3,0},{1,2},{2,1},{4,7},{7,4},{5,6},{6,5},{8,11},{11,8},{9,1... | collective-permute-start | bytes 884744 | tf_op jit(solution)/shard_map/ppermute | solution.py:215
  64.3 9.8 %collective-permute-start.22 = (bf16[48,512]{1,0:T(8,128)(2,1)S(1)}, bf16[48,512]{1,0:T(8,128)(2,1)S(1)}, u32[]{:S(2)}, u32[]{:S(2)}) collective-permute-start(bf16[48,512]{1,0:T(8,128)(2,1)S(1)} %get-tuple-element.201), channel_id=1, source_target_pairs={{0,1},{1,0},{2,3},{3,2},{4,5},{5,4},{6,7},{7,6},{8,9},{9,8},{10,11... | collective-permute-start | bytes 147464 | tf_op jit(solution)/shard_map/ppermute | solution.py:215
  64.7 21.6 %collective-permute-start.26 = (bf16[48,3072]{1,0:T(8,128)(2,1)S(1)}, bf16[48,3072]{1,0:T(8,128)(2,1)S(1)}, u32[]{:S(2)}, u32[]{:S(2)}) collective-permute-start(bf16[48,3072]{1,0:T(8,128)(2,1)S(1)} %get-tuple-element.212), channel_id=1, source_target_pairs={{0,1},{1,0},{2,3},{3,2},{4,5},{5,4},{6,7},{7,6},{8,9},{9,8},{10,11... | collective-permute-start | bytes 884744 | tf_op jit(solution)/shard_map/ppermute | solution.py:215
  64.9 22.9 %collective-permute-start.27 = (bf16[48,3072]{1,0:T(8,128)(2,1)S(1)}, bf16[48,3072]{1,0:T(8,128)(2,1)S(1)}, u32[]{:S(2)}, u32[]{:S(2)}) collective-permute-start(bf16[48,3072]{1,0:T(8,128)(2,1)S(1)} %get-tuple-element.189), channel_id=1, source_target_pairs={{0,2},{2,0},{1,3},{3,1},{4,6},{6,4},{5,7},{7,5},{8,10},{10,8},{9,1... | collective-permute-start | bytes 884744 | tf_op jit(solution)/shard_map/ppermute | solution.py:215
  66.7 21.4 %collective-permute-start.28 = (bf16[48,3072]{1,0:T(8,128)(2,1)S(1)}, bf16[48,3072]{1,0:T(8,128)(2,1)S(1)}, u32[]{:S(2)}, u32[]{:S(2)}) collective-permute-start(bf16[48,3072]{1,0:T(8,128)(2,1)S(1)} %get-tuple-element.213), channel_id=1, source_target_pairs={{0,3},{3,0},{1,2},{2,1},{4,7},{7,4},{5,6},{6,5},{8,11},{11,8},{9,1... | collective-permute-start | bytes 884744 | tf_op jit(solution)/shard_map/ppermute | solution.py:215
  72.2 4.7 %collective-permute-start.7 = (bf16[32,3072]{1,0:T(8,128)(2,1)S(1)}, bf16[32,3072]{1,0:T(8,128)(2,1)S(1)}, u32[]{:S(2)}, u32[]{:S(2)}) collective-permute-start(bf16[32,3072]{1,0:T(8,128)(2,1)S(1)} %slice.50.own.x), channel_id=1, source_target_pairs={{4,8},{8,4},{5,9},{9,5},{6,10},{10,6},{7,11},{11,7},{20,24},{24,20... | collective-permute-start | bytes 589832 | tf_op jit(solution)/shard_map/ppermute | solution.py:215
  75.6 9.1 %collective-permute-start.16 = (bf16[32,3072]{1,0:T(8,128)(2,1)S(1)}, bf16[32,3072]{1,0:T(8,128)(2,1)S(1)}, u32[]{:S(2)}, u32[]{:S(2)}) collective-permute-start(bf16[32,3072]{1,0:T(8,128)(2,1)S(1)} %collective-permute-done.6.far), channel_id=1, source_target_pairs={{4,0},{8,12},{5,1},{9,13},{6,2},{10,14},{7,3},{11,15},{20,16},{24,... | collective-permute-start | bytes 589832 | tf_op jit(solution)/shard_map/ppermute | solution.py:215
  77.0 11.9 %collective-permute-start.25 = (bf16[96,512]{1,0:T(8,128)(2,1)S(1)}, bf16[96,512]{1,0:T(8,128)(2,1)S(1)}, u32[]{:S(2)}, u32[]{:S(2)}) collective-permute-start(bf16[96,512]{1,0:T(8,128)(2,1)S(1)} %get-tuple-element.211), channel_id=1, source_target_pairs={{0,2},{2,0},{1,3},{3,1},{4,6},{6,4},{5,7},{7,5},{8,10},{10,8},{9,1... | collective-permute-start | bytes 294920 | tf_op jit(solution)/shard_map/ppermute | solution.py:215
  86.2 7.8 %collective-permute-start.24 = (bf16[32,3072]{1,0:T(8,128)(2,1)S(1)}, bf16[32,3072]{1,0:T(8,128)(2,1)S(1)}, u32[]{:S(2)}, u32[]{:S(2)}) collective-permute-start(bf16[32,3072]{1,0:T(8,128)(2,1)S(1)} %get-tuple-element.210), channel_id=1, source_target_pairs={{0,1},{1,0},{2,3},{3,2},{4,5},{5,4},{6,7},{7,6},{8,9},{9,8},{10,11... | collective-permute-start | bytes 589832 | tf_op jit(solution)/shard_map/ppermute | solution.py:215
  86.3 8.9 %collective-permute-start.30 = (bf16[32,3072]{1,0:T(8,128)(2,1)S(1)}, bf16[32,3072]{1,0:T(8,128)(2,1)S(1)}, u32[]{:S(2)}, u32[]{:S(2)}) collective-permute-start(bf16[32,3072]{1,0:T(8,128)(2,1)S(1)} %get-tuple-element.227), channel_id=1, source_target_pairs={{0,2},{2,0},{1,3},{3,1},{4,6},{6,4},{5,7},{7,5},{8,10},{10,8},{9,1... | collective-permute-start | bytes 589832 | tf_op jit(solution)/shard_map/ppermute | solution.py:215
  87.8 9.6 %collective-permute-start.31 = (bf16[32,3072]{1,0:T(8,128)(2,1)S(1)}, bf16[32,3072]{1,0:T(8,128)(2,1)S(1)}, u32[]{:S(2)}, u32[]{:S(2)}) collective-permute-start(bf16[32,3072]{1,0:T(8,128)(2,1)S(1)} %get-tuple-element.228), channel_id=1, source_target_pairs={{0,3},{3,0},{1,2},{2,1},{4,7},{7,4},{5,6},{6,5},{8,11},{11,8},{9,1... | collective-permute-start | bytes 589832 | tf_op jit(solution)/shard_map/ppermute | solution.py:215
  89.9 12.1 %collective-permute-start.38 = (bf16[48,3072]{1,0:T(8,128)(2,1)S(1)}, bf16[48,3072]{1,0:T(8,128)(2,1)S(1)}, u32[]{:S(2)}, u32[]{:S(2)}) collective-permute-start(bf16[48,3072]{1,0:T(8,128)(2,1)S(1)} %get-tuple-element.239), channel_id=1, source_target_pairs={{0,4},{12,8},{1,5},{13,9},{2,6},{14,10},{3,7},{15,11},{16,20},{28,... | collective-permute-start | bytes 884744 | tf_op jit(solution)/shard_map/ppermute | solution.py:215
  97.3 3.9 %collective-permute-start.32 = (bf16[32,512]{1,0:T(8,128)(2,1)S(1)}, bf16[32,512]{1,0:T(8,128)(2,1)S(1)}, u32[]{:S(2)}, u32[]{:S(2)}) collective-permute-start(bf16[32,512]{1,0:T(8,128)(2,1)S(1)} %get-tuple-element.232), channel_id=1, source_target_pairs={{0,1},{1,0},{2,3},{3,2},{4,5},{5,4},{6,7},{7,6},{8,9},{9,8},{10,11... | collective-permute-start | bytes 98312 | tf_op jit(solution)/shard_map/ppermute | solution.py:215
  98.8 2.4 %collective-permute-start.33 = (bf16[32,512]{1,0:T(8,128)(2,1)S(1)}, bf16[32,512]{1,0:T(8,128)(2,1)S(1)}, u32[]{:S(2)}, u32[]{:S(2)}) collective-permute-start(bf16[32,512]{1,0:T(8,128)(2,1)S(1)} %get-tuple-element.233), channel_id=1, source_target_pairs={{0,1},{1,0},{2,3},{3,2},{4,5},{5,4},{6,7},{7,6},{8,9},{9,8},{10,11... | collective-permute-start | bytes 98312 | tf_op jit(solution)/shard_map/ppermute | solution.py:215
  99.0 24.6 %collective-permute-start.44 = (bf16[48,3072]{1,0:T(8,128)(2,1)S(1)}, bf16[48,3072]{1,0:T(8,128)(2,1)S(1)}, u32[]{:S(2)}, u32[]{:S(2)}) collective-permute-start(bf16[48,3072]{1,0:T(8,128)(2,1)S(1)} %get-tuple-element.239), channel_id=1, source_target_pairs={{4,8},{8,4},{5,9},{9,5},{6,10},{10,6},{7,11},{11,7},{20,24},{24,20... | collective-permute-start | bytes 884744 | tf_op jit(solution)/shard_map/ppermute | solution.py:215
  99.7 9.9 %collective-permute-start.36 = (bf16[48,3072]{1,0:T(8,128)(2,1)S(1)}, bf16[48,3072]{1,0:T(8,128)(2,1)S(1)}, u32[]{:S(2)}, u32[]{:S(2)}) collective-permute-start(bf16[48,3072]{1,0:T(8,128)(2,1)S(1)} %get-tuple-element.220), channel_id=1, source_target_pairs={{0,2},{2,0},{1,3},{3,1},{4,6},{6,4},{5,7},{7,5},{8,10},{10,8},{9,1... | collective-permute-start | bytes 884744 | tf_op jit(solution)/shard_map/ppermute | solution.py:215
  101.2 13.7 %collective-permute-start.37 = (bf16[48,3072]{1,0:T(8,128)(2,1)S(1)}, bf16[48,3072]{1,0:T(8,128)(2,1)S(1)}, u32[]{:S(2)}, u32[]{:S(2)}) collective-permute-start(bf16[48,3072]{1,0:T(8,128)(2,1)S(1)} %get-tuple-element.237), channel_id=1, source_target_pairs={{0,3},{3,0},{1,2},{2,1},{4,7},{7,4},{5,6},{6,5},{8,11},{11,8},{9,1... | collective-permute-start | bytes 884744 | tf_op jit(solution)/shard_map/ppermute | solution.py:215
  101.9 14.7 %collective-permute-start.34 = (bf16[64,512]{1,0:T(8,128)(2,1)S(1)}, bf16[64,512]{1,0:T(8,128)(2,1)S(1)}, u32[]{:S(2)}, u32[]{:S(2)}) collective-permute-start(bf16[64,512]{1,0:T(8,128)(2,1)S(1)} %get-tuple-element.235), channel_id=1, source_target_pairs={{0,2},{2,0},{1,3},{3,1},{4,6},{6,4},{5,7},{7,5},{8,10},{10,8},{9,1... | collective-permute-start | bytes 196616 | tf_op jit(solution)/shard_map/ppermute | solution.py:215
  103.5 21.6 %collective-permute-start.45 = (bf16[48,3072]{1,0:T(8,128)(2,1)S(1)}, bf16[48,3072]{1,0:T(8,128)(2,1)S(1)}, u32[]{:S(2)}, u32[]{:S(2)}) collective-permute-start(bf16[48,3072]{1,0:T(8,128)(2,1)S(1)} %get-tuple-element.256), channel_id=1, source_target_pairs={{0,4},{4,0},{8,12},{12,8},{1,5},{5,1},{9,13},{13,9},{2,6},{6,2},{1... | collective-permute-start | bytes 884744 | tf_op jit(solution)/shard_map/ppermute | solution.py:215
  109.6 15.5 %collective-permute-start.46 = (bf16[48,3072]{1,0:T(8,128)(2,1)S(1)}, bf16[48,3072]{1,0:T(8,128)(2,1)S(1)}, u32[]{:S(2)}, u32[]{:S(2)}) collective-permute-start(bf16[48,3072]{1,0:T(8,128)(2,1)S(1)} %add_convert_fusion.1), channel_id=1, source_target_pairs={{0,8},{8,0},{4,12},{12,4},{1,9},{9,1},{5,13},{13,5},{2,10},{10,2},... | collective-permute-start | bytes 884744 | tf_op jit(solution)/shard_map/ppermute | solution.py:215
  117.3 3.2 %collective-permute-start.39 = (bf16[64,512]{1,0:T(8,128)(2,1)S(1)}, bf16[64,512]{1,0:T(8,128)(2,1)S(1)}, u32[]{:S(2)}, u32[]{:S(2)}) collective-permute-start(bf16[64,512]{1,0:T(8,128)(2,1)S(1)} %shard_map.113), channel_id=1, source_target_pairs={{0,1},{1,0},{2,3},{3,2},{4,5},{5,4},{6,7},{7,6},{8,9},{9,8},{10,11... | collective-permute-start | bytes 196616 | tf_op jit(solution)/shard_map/ppermute | solution.py:215
  117.4 9.8 %collective-permute-start.43 = (bf16[48,3072]{1,0:T(8,128)(2,1)S(1)}, bf16[48,3072]{1,0:T(8,128)(2,1)S(1)}, u32[]{:S(2)}, u32[]{:S(2)}) collective-permute-start(bf16[48,3072]{1,0:T(8,128)(2,1)S(1)} %get-tuple-element.254), channel_id=1, source_target_pairs={{0,4},{12,8},{1,5},{13,9},{2,6},{14,10},{3,7},{15,11},{16,20},{28,... | collective-permute-start | bytes 884744 | tf_op jit(solution)/shard_map/ppermute | solution.py:215
  120.5 19.0 %collective-permute-start.50 = (bf16[48,3072]{1,0:T(8,128)(2,1)S(1)}, bf16[48,3072]{1,0:T(8,128)(2,1)S(1)}, u32[]{:S(2)}, u32[]{:S(2)}) collective-permute-start(bf16[48,3072]{1,0:T(8,128)(2,1)S(1)} %get-tuple-element.254), channel_id=1, source_target_pairs={{4,8},{8,4},{5,9},{9,5},{6,10},{10,6},{7,11},{11,7},{20,24},{24,20... | collective-permute-start | bytes 884744 | tf_op jit(solution)/shard_map/ppermute | solution.py:215
  123.6 7.8 %collective-permute-start.41 = (bf16[32,3072]{1,0:T(8,128)(2,1)S(1)}, bf16[32,3072]{1,0:T(8,128)(2,1)S(1)}, u32[]{:S(2)}, u32[]{:S(2)}) collective-permute-start(bf16[32,3072]{1,0:T(8,128)(2,1)S(1)} %get-tuple-element.247), channel_id=1, source_target_pairs={{0,2},{2,0},{1,3},{3,1},{4,6},{6,4},{5,7},{7,5},{8,10},{10,8},{9,1... | collective-permute-start | bytes 589832 | tf_op jit(solution)/shard_map/ppermute | solution.py:215
  125.1 4.7 %collective-permute-start.40 = (bf16[32,3072]{1,0:T(8,128)(2,1)S(1)}, bf16[32,3072]{1,0:T(8,128)(2,1)S(1)}, u32[]{:S(2)}, u32[]{:S(2)}) collective-permute-start(bf16[32,3072]{1,0:T(8,128)(2,1)S(1)} %get-tuple-element.251), channel_id=1, source_target_pairs={{0,1},{1,0},{2,3},{3,2},{4,5},{5,4},{6,7},{7,6},{8,9},{9,8},{10,11... | collective-permute-start | bytes 589832 | tf_op jit(solution)/shard_map/ppermute | solution.py:215
  125.1 8.8 %collective-permute-start.42 = (bf16[32,3072]{1,0:T(8,128)(2,1)S(1)}, bf16[32,3072]{1,0:T(8,128)(2,1)S(1)}, u32[]{:S(2)}, u32[]{:S(2)}) collective-permute-start(bf16[32,3072]{1,0:T(8,128)(2,1)S(1)} %get-tuple-element.252), channel_id=1, source_target_pairs={{0,3},{3,0},{1,2},{2,1},{4,7},{7,4},{5,6},{6,5},{8,11},{11,8},{9,1... | collective-permute-start | bytes 589832 | tf_op jit(solution)/shard_map/ppermute | solution.py:215
  127.2 15.4 %collective-permute-start.51 = (bf16[48,3072]{1,0:T(8,128)(2,1)S(1)}, bf16[48,3072]{1,0:T(8,128)(2,1)S(1)}, u32[]{:S(2)}, u32[]{:S(2)}) collective-permute-start(bf16[48,3072]{1,0:T(8,128)(2,1)S(1)} %get-tuple-element.271), channel_id=1, source_target_pairs={{0,4},{4,0},{8,12},{12,8},{1,5},{5,1},{9,13},{13,9},{2,6},{6,2},{1... | collective-permute-start | bytes 884744 | tf_op jit(solution)/shard_map/ppermute | solution.py:215
  129.8 14.3 %collective-permute-start.52 = (bf16[48,3072]{1,0:T(8,128)(2,1)S(1)}, bf16[48,3072]{1,0:T(8,128)(2,1)S(1)}, u32[]{:S(2)}, u32[]{:S(2)}) collective-permute-start(bf16[48,3072]{1,0:T(8,128)(2,1)S(1)} %add_convert_fusion), channel_id=1, source_target_pairs={{0,8},{8,0},{4,12},{12,4},{1,9},{9,1},{5,13},{13,5},{2,10},{10,2},... | collective-permute-start | bytes 884744 | tf_op jit(solution)/shard_map/ppermute | solution.py:215
  134.5 13.2 %collective-permute-start.49 = (bf16[32,3072]{1,0:T(8,128)(2,1)S(1)}, bf16[32,3072]{1,0:T(8,128)(2,1)S(1)}, u32[]{:S(2)}, u32[]{:S(2)}) collective-permute-start(bf16[32,3072]{1,0:T(8,128)(2,1)S(1)} %get-tuple-element.267), channel_id=1, source_target_pairs={{0,4},{12,8},{1,5},{13,9},{2,6},{14,10},{3,7},{15,11},{16,20},{28,... | collective-permute-start | bytes 589832 | tf_op jit(solution)/shard_map/ppermute | solution.py:215
  138.8 12.7 %collective-permute-start.47 = (bf16[32,3072]{1,0:T(8,128)(2,1)S(1)}, bf16[32,3072]{1,0:T(8,128)(2,1)S(1)}, u32[]{:S(2)}, u32[]{:S(2)}) collective-permute-start(bf16[32,3072]{1,0:T(8,128)(2,1)S(1)} %get-tuple-element.267), channel_id=1, source_target_pairs={{4,8},{8,4},{5,9},{9,5},{6,10},{10,6},{7,11},{11,7},{20,24},{24,20... | collective-permute-start | bytes 589832 | tf_op jit(solution)/shard_map/ppermute | solution.py:215
  139.5 12.5 %collective-permute-start.48 = (bf16[32,3072]{1,0:T(8,128)(2,1)S(1)}, bf16[32,3072]{1,0:T(8,128)(2,1)S(1)}, u32[]{:S(2)}, u32[]{:S(2)}) collective-permute-start(bf16[32,3072]{1,0:T(8,128)(2,1)S(1)} %get-tuple-element.268), channel_id=1, source_target_pairs={{0,4},{4,0},{8,12},{12,8},{1,5},{5,1},{9,13},{13,9},{2,6},{6,2},{1... | collective-permute-start | bytes 589832 | tf_op jit(solution)/shard_map/ppermute | solution.py:215
  147.8 11.1 %collective-permute-start.53 = (bf16[32,3072]{1,0:T(8,128)(2,1)S(1)}, bf16[32,3072]{1,0:T(8,128)(2,1)S(1)}, u32[]{:S(2)}, u32[]{:S(2)}) collective-permute-start(bf16[32,3072]{1,0:T(8,128)(2,1)S(1)} %add_convert_fusion.2), channel_id=1, source_target_pairs={{0,8},{8,0},{4,12},{12,4},{1,9},{9,1},{5,13},{13,5},{2,10},{10,2},... | collective-permute-start | bytes 589832 | tf_op jit(solution)/shard_map/ppermute | solution.py:215
  (7 other events, 17.4 us)
